TPU v7x, 32 devices: a whole 2x2x4 slice. The times are simulated.
32 devices in a mesh: row: 8 (over z, y), col: 4 (over x, core).
Axes of the slice: x: 2, y: 2, z: 4, core: 2. Of those that a mesh axis runs over, the one named last changes fastest.
Arguments:
- embeddings: bfloat16 [512, 256], P(('row', 'col')), may hold values from -6 to 6
- labels: bfloat16 [512, 1024], P(('row', 'col')), may hold values from -6 to 6
- tile_mask: int32 [2, 2], replicated, may hold values 0 or 1
Outputs:
- spread_labels: bfloat16 [512, 1024], P(('row', 'col'))
Inputs may be any that keep to these rules, and one draw needn't show every extreme that they name: Only the entries tile_mask[i, j] with i < j are read; the tile of blocks i and j (and of j and i) is kept where it is 1.
All inputs are finite; a program needn't handle non-finite values.
Results may differ from a plain program's by a relative error of at most 0.015.
Values may be sent and summed in bfloat16 or wider, within the bound.
No kernel may reach another device: no remote copies, remote signals or barrier semaphores. Data moves between devices by JAX's collectives and lax.ppermute only.
A program may use at most 64 MiB of HBM per device.

v0:
```python
import math

import jax
import jax.numpy as jnp
from jax import lax
from jax.sharding import PartitionSpec as P

BLOCK = 256
ITERS = 2


MIXING = 0.9
SHARPNESS = 3.0
EPSILON = 1e-06


def unit_rows(embeddings):
    values = embeddings.astype(jnp.float32)
    return (values * lax.rsqrt(jnp.sum(values * values, axis=1, keepdims=True) + EPSILON)).astype(
        jnp.bfloat16
    )


def symmetric_keep(tile_mask):
    blocks = tile_mask.shape[0]
    block_row = lax.broadcasted_iota(jnp.int32, (blocks, blocks), 0)
    block_col = lax.broadcasted_iota(jnp.int32, (blocks, blocks), 1)
    mirrored = jnp.where(block_row < block_col, tile_mask, tile_mask.T)
    return (jnp.where(block_row == block_col, 1, mirrored), block_row, block_col)


def rotate_rows(values, start):
    total = values.shape[0]
    doubled = jnp.concatenate([values, values], axis=0)
    return lax.dynamic_slice_in_dim(doubled, start, total, 0)


def one_term(operands):
    row_kernel, part_labels = operands
    return jnp.dot(row_kernel, part_labels, preferred_element_type=jnp.float32)


def no_term(operands):
    row_kernel, part_labels = operands
    return jnp.zeros((row_kernel.shape[0], part_labels.shape[1]), jnp.float32)


def shards(embeddings, labels, tile_mask):
    row_count = lax.axis_size("row")
    col_count = lax.axis_size("col")
    row_index = lax.axis_index("row")
    col_index = lax.axis_index("col")
    piece_rows = embeddings.shape[0]
    emb_width = embeddings.shape[1]
    channels = labels.shape[1]
    blocks = tile_mask.shape[0]
    sharpness = SHARPNESS * math.sqrt(emb_width)
    unit_vecs = unit_rows(embeddings)
    row_units = lax.all_gather(unit_vecs, "col", axis=0, tiled=True)
    col_gathered = lax.all_gather(unit_vecs, "row", axis=0, tiled=True)
    row_total = row_units.shape[0]
    col_total = col_gathered.shape[0]
    shift = row_index * piece_rows
    col_units = rotate_rows(col_gathered, shift)
    unit_count = math.gcd(8, row_count)
    unit_width = col_total // unit_count
    kept_sym, block_row, block_col = symmetric_keep(tile_mask)
    global_rows = row_index * row_total + jnp.arange(row_total, dtype=jnp.int32)
    row_blocks = global_rows // BLOCK
    block_ids = jnp.arange(blocks, dtype=jnp.int32)
    row_onehot = (row_blocks[:, None] == block_ids[None, :]).astype(jnp.bfloat16)
    row_table = jnp.dot(
        row_onehot, kept_sym.astype(jnp.bfloat16), preferred_element_type=jnp.float32
    ).astype(jnp.bfloat16)
    local_cols = (jnp.arange(col_total, dtype=jnp.int32) + shift) % col_total
    global_cols = (
        local_cols // piece_rows * col_count + col_index
    ) * piece_rows + local_cols % piece_rows
    col_blocks = global_cols // BLOCK
    kernels_row = []
    active_flags = []
    row_degree = jnp.zeros((row_total,), jnp.float32)
    for column_unit in range(unit_count):
        offset_cols = column_unit * unit_width
        part_units = col_units[offset_cols : offset_cols + unit_width]
        part_blocks = col_blocks[offset_cols : offset_cols + unit_width]
        part_cols = global_cols[offset_cols : offset_cols + unit_width]
        col_onehot = (part_blocks[:, None] == block_ids[None, :]).astype(jnp.bfloat16)
        kept_mask = lax.dot_general(
            row_table, col_onehot, (((1,), (1,)), ((), ())), preferred_element_type=jnp.float32
        )
        cosine = lax.dot_general(
            row_units, part_units, (((1,), (1,)), ((), ())), preferred_element_type=jnp.float32
        )
        distinct = global_rows[:, None] != part_cols[None, :]
        weights = jnp.where(
            distinct, jnp.exp(sharpness * cosine) * kept_mask, jnp.zeros_like(cosine)
        ).astype(jnp.bfloat16)
        active_flags.append(jnp.sum(kept_mask) > 0.0)
        kernels_row.append(weights)
        row_degree = row_degree + jnp.sum(weights, axis=1, dtype=jnp.float32)
    degree = lax.psum_scatter(row_degree, "col", scatter_dimension=0, tiled=True)
    inv_root = lax.rsqrt(degree)
    seed_scores = labels.astype(jnp.float32)
    current = seed_scores
    for iteration in range(ITERS):
        scaled = (inv_root[:, None] * current).astype(jnp.bfloat16)
        col_labels = rotate_rows(lax.all_gather(scaled, "row", axis=0, tiled=True), shift)
        row_sum = jnp.zeros((row_total, channels), jnp.float32)
        for column_unit in range(unit_count):
            offset_cols = column_unit * unit_width
            part_labels = col_labels[offset_cols : offset_cols + unit_width]
            row_sum = row_sum + lax.cond(
                active_flags[column_unit],
                one_term,
                no_term,
                (kernels_row[column_unit], part_labels),
            )
        sent_rows = row_sum.astype(jnp.bfloat16).reshape(col_count, piece_rows, channels)
        arrived = lax.all_to_all(sent_rows, "col", split_axis=0, concat_axis=0, tiled=True)
        spread = jnp.sum(arrived, axis=0, dtype=jnp.float32)
        current = MIXING * inv_root[:, None] * spread + (1.0 - MIXING) * seed_scores
    return current.astype(jnp.bfloat16)


def solution(mesh):
    placed = (P(("row", "col"), None), P(("row", "col"), None), P())
    return jax.shard_map(
        shards, mesh=mesh, in_specs=placed, out_specs=P(("row", "col"), None), check_vma=False
    )
```

profile of v0, /device:TPU:0, one launch (start us, length us, event | category | flops | bytes accessed | tf_op | source)
XLA Modules:
  0.0 143.4 jit_solution(3231743709435597524)
XLA Ops:
  0.0 0.7 copy-done.1
  0.9 6.2 %all_gather.12 = bf16[64,256]{1,0:T(8,128)(2,1)S(1)} all-gather(bf16[16,256]{1,0:T(8,128)(2,1)S(1)} %fusion.74), channel_id=1, replica_groups=mesh['row'=8,'col'=4] {'col'}, dimensions={0}, use_global_device_ids=true | all-gather | bytes 40960 | tf_op jit(solution)/shard_map/all_gather | solution.py:59
  7.1 31.3 %all_gather.13 = bf16[128,256]{1,0:T(8,128)(2,1)S(1)} all-gather(bf16[16,256]{1,0:T(8,128)(2,1)S(1)} %fusion.74), channel_id=1, replica_groups=mesh['row'=8,'col'=4] {'row'}, dimensions={0}, use_global_device_ids=true | all-gather | bytes 73728 | tf_op jit(solution)/shard_map/all_gather | solution.py:60
  38.4 0.6 copy-done.2
  39.3 0.2 convolution_convert_fusion
  39.5 0.8 fusion.115
  40.9 0.8 fusion.108
  42.4 0.9 fusion.109
  43.9 0.9 fusion.110
  45.5 0.9 fusion.111
  47.1 0.9 fusion.112
  48.6 0.9 fusion.113
  50.2 0.9 fusion.114
  53.2 5.7 %all-reduce = f32[64]{0:T(128)S(1)} all-reduce(f32[64]{0:T(128)S(1)} %add_add_fusion), channel_id=2, replica_groups=mesh['row'=8,'col'=4] {'col'}, use_global_device_ids=true, to_apply=%region_9.10.clone | all-reduce | flops 64 | bytes 512
  58.9 0.7 copy-done.3
  59.5 0.7 dynamic-slice
  61.0 30.7 %all_gather.14 = bf16[128,1024]{1,0:T(8,128)(2,1)S(1)} all-gather(bf16[16,1024]{1,0:T(8,128)(2,1)S(1)} %fusion.71), channel_id=1, replica_groups=mesh['row'=8,'col'=4] {'row'}, dimensions={0}, use_global_device_ids=true | all-gather | bytes 294912 | tf_op jit(solution)/shard_map/all_gather | solution.py:108
  91.9 0.2 conditional.23
  92.0 0.2 fusion.14
  92.2 0.2 conditional.16
  92.4 0.2 conditional.17
  92.6 0.2 conditional.18
  92.7 0.2 fusion.4
  92.9 0.2 conditional.19
  92.9 0.2 fusion.6
  93.1 0.2 conditional.20
  93.3 0.2 conditional.21
  93.3 0.2 fusion.10
  93.6 0.2 conditional.22
  93.6 0.2 fusion.12
  93.8 0.8 add_convert_fusion.1
  94.6 3.3 %all-to-all-start = ((bf16[4,16,1024]{2,1,0:T(8,128)(2,1)}), bf16[4,16,1024]{2,1,0:T(8,128)(2,1)S(1)}, u32[]{:S(2)}, u32[]{:S(2)}) async-start(bf16[4,16,1024]{2,1,0:T(8,128)(2,1)} %bitcast.1), calls=%async_computation | async-start | bytes 262144 | tf_op jit(solution)/shard_map/all_to_all | solution.py:120
  97.9 4.6 %all-to-all-done = bf16[4,16,1024]{2,1,0:T(8,128)(2,1)S(1)} async-done(((bf16[4,16,1024]{2,1,0:T(8,128)(2,1)}), bf16[4,16,1024]{2,1,0:T(8,128)(2,1)S(1)}, u32[]{:S(2)}, u32[]{:S(2)}) %all-to-all-start) | async-done | bytes 131104 | tf_op jit(solution)/shard_map/all_to_all | solution.py:120
  102.6 30.9 %all_gather.15 = bf16[128,1024]{1,0:T(8,128)(2,1)S(1)} all-gather(bf16[16,1024]{1,0:T(8,128)(2,1)S(1)} %fusion.69), channel_id=1, replica_groups=mesh['row'=8,'col'=4] {'row'}, dimensions={0}, use_global_device_ids=true | all-gather | bytes 294912 | tf_op jit(solution)/shard_map/all_gather | solution.py:108
  133.7 0.2 conditional.31
  133.7 0.2 fusion.30
  133.9 0.2 conditional.24
  134.1 0.2 conditional.25
  134.3 0.2 conditional.26
  134.4 0.2 fusion.20
  134.6 0.2 conditional.27
  134.6 0.2 fusion.22
  134.8 0.2 conditional.28
  135.0 0.2 conditional.29
  135.1 0.2 fusion.26
  135.3 0.2 conditional.30
  135.7 7.0 %all_to_all.10 = bf16[4,16,1024]{2,1,0:T(8,128)(2,1)S(1)} all-to-all(bf16[4,16,1024]{2,1,0:T(8,128)(2,1)S(1)} %bitcast.38), channel_id=1, replica_groups=mesh['row'=8,'col'=4] {'col'}, dimensions={0} | all-to-all | bytes 262144 | tf_op jit(solution)/shard_map/all_to_all | solution.py:120
  142.7 0.7 fusion.70
  (39 shorter events, 4.0 us)
Async XLA Ops:
  0.0 0.7 copy-start.1
  38.4 0.7 copy-start.2
  53.2 7.8 %copy-start = (bf16[16,1024]{1,0:T(8,128)(2,1)S(1)}, bf16[16,1024]{1,0:T(8,128)(2,1)}, u32[]{:S(2)}) copy-start(bf16[16,1024]{1,0:T(8,128)(2,1)} %param.36) | copy-start | bytes 98308
  58.9 0.7 copy-start.3
  94.6 7.9 %all-to-all-start = ((bf16[4,16,1024]{2,1,0:T(8,128)(2,1)}), bf16[4,16,1024]{2,1,0:T(8,128)(2,1)S(1)}, u32[]{:S(2)}, u32[]{:S(2)}) async-start(bf16[4,16,1024]{2,1,0:T(8,128)(2,1)} %bitcast.1), calls=%async_computation | async-start | bytes 262144 | tf_op jit(solution)/shard_map/all_to_all | solution.py:120
where the time goes:
time: 143 us
  blocking collectives  112 us (78%)
  matrix products  11.4 us (8%)
  between operations  6.46 us (5%)
  waiting for transfers between devices  4.6 us (3%)
  starting transfers between devices  3.32 us (2%)
  local copies, waits for them, and re-layouts  2.9 us (2%)
  other arithmetic  2.57 us (2%)
    all_gather x2, blocking collectives, shards(): lax.all_gather(scaled, 'row', axis=0, tiled=True)  61.6 us
    all_gather x1, blocking collectives, shards(): col_gathered = lax.all_gather(unit_vecs, 'row', axis=0, tiled=True)  31.3 us
    all_to_all x1, blocking collectives, shards(): lax.all_to_all(sent_rows, 'col', split_axis=0, concat_axis=0, tiled=True)  7.02 us
    dot_general x8, matrix products, shards(): lax.dot_general(row_table, col_onehot, (((1,), (1,)), ((), ())), preferre...  6.79 us
    all_gather x1, blocking collectives, shards(): row_units = lax.all_gather(unit_vecs, 'col', axis=0, tiled=True)  6.17 us
    unnamed x1, blocking collectives  5.67 us
    all_to_all x1, waiting for transfers between devices, shards(): lax.all_to_all(sent_rows, 'col', split_axis=0, concat_axis=0, tiled=True)  4.6 us
    all_to_all x1, starting transfers between devices, shards(): lax.all_to_all(sent_rows, 'col', split_axis=0, concat_axis=0, tiled=True)  3.32 us
  transfers between devices with their start and end apart: 1, of which 1 were waited for; matrix products, arithmetic and copies ran while one was open for 0% of the time, Pallas kernels for 0%

commit v1 on v0

--- a/solution.py
+++ b/solution.py
@@ -1,8 +1,11 @@
+import functools
 import math
 
 import jax
 import jax.numpy as jnp
 from jax import lax
+from jax.experimental import pallas as pl
+from jax.experimental.pallas import tpu as pltpu
 from jax.sharding import PartitionSpec as P
 
 BLOCK = 256
@@ -123,8 +126,129 @@
     return current.astype(jnp.bfloat16)
 
 
+AXES = ("row", "col")
+LANES = 128
+WHOLE_KERNEL_BYTES = 4 * 1024 * 1024
+
+
+def pack_body(emb_ref, lab_ref, sent_ref):
+    peers, _, width = sent_ref.shape
+    emb_width = emb_ref.shape[1]
+    lanes = width - emb_width
+    near = lab_ref.shape[1] // lanes
+    unit_vecs = unit_rows(emb_ref[...])
+    for peer in range(peers):
+        first = peer % near * lanes
+        sent_ref[peer, :, :emb_width] = unit_vecs
+        sent_ref[peer, :, emb_width:] = lab_ref[:, first : first + lanes]
+
+
+def spread_body(emb_width, mask_ref, start_ref, all_ref, out_ref, kernel_ref):
+    images = all_ref.shape[0]
+    lanes = out_ref.shape[1]
+    blocks = images // BLOCK
+    sharpness = SHARPNESS * math.sqrt(emb_width)
+    for i in range(blocks):
+        rows = slice(i * BLOCK, (i + 1) * BLOCK)
+        for j in range(blocks):
+            cols = slice(j * BLOCK, (j + 1) * BLOCK)
+            cosine = lax.dot_general(
+                all_ref[rows, :emb_width],
+                all_ref[cols, :emb_width],
+                (((1,), (1,)), ((), ())),
+                preferred_element_type=jnp.float32,
+            )
+            weights = jnp.exp(sharpness * cosine)
+            if i == j:
+                row_ids = lax.broadcasted_iota(jnp.int32, weights.shape, 0)
+                col_ids = lax.broadcasted_iota(jnp.int32, weights.shape, 1)
+                weights = jnp.where(row_ids == col_ids, 0.0, weights)
+            else:
+                weights = weights * mask_ref[min(i, j), max(i, j)].astype(jnp.float32)
+            kernel_ref[rows, cols] = weights.astype(jnp.bfloat16)
+    labels = all_ref[:, emb_width:].astype(jnp.float32)
+    weights = kernel_ref[...]
+    degree = jnp.dot(
+        weights, jnp.ones((images, lanes), jnp.bfloat16), preferred_element_type=jnp.float32
+    )
+    inv_root = lax.rsqrt(degree)
+    current = labels
+    for iteration in range(ITERS - 1):
+        scaled = (inv_root * current).astype(jnp.bfloat16)
+        spread = jnp.dot(weights, scaled, preferred_element_type=jnp.float32)
+        current = MIXING * inv_root * spread + (1.0 - MIXING) * labels
+    scaled = (inv_root * current).astype(jnp.bfloat16)
+    own_rows = pl.ds(pl.multiple_of(start_ref[0], 16), out_ref.shape[0])
+    own_weights = kernel_ref[own_rows, :]
+    own_degree = jnp.dot(
+        own_weights, jnp.ones((images, lanes), jnp.bfloat16), preferred_element_type=jnp.float32
+    )
+    spread = jnp.dot(own_weights, scaled, preferred_element_type=jnp.float32)
+    own_labels = all_ref[own_rows, emb_width:].astype(jnp.float32)
+    out_ref[...] = (
+        MIXING * lax.rsqrt(own_degree) * spread + (1.0 - MIXING) * own_labels
+    ).astype(jnp.bfloat16)
+
+
+def whole_shards(embeddings, labels, tile_mask):
+    piece_rows, emb_width = embeddings.shape
+    channels = labels.shape[1]
+    lanes = LANES
+    near = channels // lanes
+    peers = lax.axis_size(AXES)
+    groups = [list(range(first, first + near)) for first in range(0, peers, near)]
+    images = peers * piece_rows
+    width = emb_width + lanes
+    vmem = pl.BlockSpec(memory_space=pltpu.VMEM)
+    smem = pl.BlockSpec(memory_space=pltpu.SMEM)
+    sent = pl.pallas_call(
+        pack_body,
+        out_shape=jax.ShapeDtypeStruct((peers, piece_rows, width), jnp.bfloat16),
+        in_specs=[vmem, vmem],
+        out_specs=vmem,
+    )(embeddings, labels)
+    arrived = lax.all_to_all(sent, AXES, split_axis=0, concat_axis=0, tiled=True)
+    group_rows = near * piece_rows
+    start = (lax.axis_index(AXES) // near * group_rows).astype(jnp.int32).reshape(1)
+    group_out = pl.pallas_call(
+        functools.partial(spread_body, emb_width),
+        out_shape=jax.ShapeDtypeStruct((group_rows, lanes), jnp.bfloat16),
+        in_specs=[smem, smem, vmem],
+        out_specs=vmem,
+        scratch_shapes=[pltpu.VMEM((images, images), jnp.bfloat16)],
+        compiler_params=pltpu.CompilerParams(vmem_limit_bytes=32 * 1024 * 1024),
+    )(tile_mask, start, arrived.reshape(images, width))
+    pieces = lax.all_to_all(
+        group_out.reshape(near, piece_rows, lanes),
+        AXES,
+        split_axis=0,
+        concat_axis=0,
+        axis_index_groups=groups,
+        tiled=True,
+    )
+    return pieces.transpose(1, 0, 2).reshape(piece_rows, channels)
+
+
 def solution(mesh):
-    placed = (P(("row", "col"), None), P(("row", "col"), None), P())
-    return jax.shard_map(
-        shards, mesh=mesh, in_specs=placed, out_specs=P(("row", "col"), None), check_vma=False
-    )
+    placed = (P(AXES, None), P(AXES, None), P())
+    devices = mesh.devices.size
+
+    def spread_labels(embeddings, labels, tile_mask):
+        images = embeddings.shape[0]
+        channels = labels.shape[1]
+        whole = (
+            images * images * 2 <= WHOLE_KERNEL_BYTES
+            and images % (devices * 16) == 0
+            and images % BLOCK == 0
+            and channels % LANES == 0
+            and devices % (channels // LANES) == 0
+        )
+        return jax.shard_map(
+            whole_shards if whole else shards,
+            mesh=mesh,
+            in_specs=placed,
+            out_specs=P(AXES, None),
+            check_vma=False,
+        )(embeddings, labels, tile_mask)
+
+    return spread_labels

time: 143 us -> 32.8 us (0.23)
  blocking collectives: 112 us -> 7.34 us
  matrix products: 11.4 us -> 0 us
  waiting for transfers between devices: 4.6 us -> 13.2 us
  between operations: 6.46 us -> 0.03 us
  starting transfers between devices: 3.32 us -> 7.3 us
  Pallas kernels: 0 us -> 3.3 us
  other arithmetic: 2.57 us -> 0 us
  local copies, waits for them, and re-layouts: 2.9 us -> 1.3 us
    all_gather x4 -> x0, blocking collectives: 99.1 us -> none  [the longest x2 61.6 us: shards(): lax.all_gather(scaled, 'row', axis=0, tiled=True)]
    dot_general x33 -> x0, matrix products: 11.4 us -> none  [the longest x8 6.79 us: shards(): lax.dot_general(row_table, col_onehot, (((1,), (1,)), ((), ())), preferre...]
    all_to_all x1, waiting for transfers between devices: 4.6 us -> 13.2 us  [whole_shards(): lax.all_to_all(sent, AXES, split_axis=0, concat_axis=0, tiled=True)]
    unnamed x1 -> x0, blocking collectives: 5.67 us -> none
    all_to_all x1, starting transfers between devices: 3.32 us -> 7.3 us  [whole_shards(): lax.all_to_all(sent, AXES, split_axis=0, concat_axis=0, tiled=True)]
    pallas_call x0 -> x2, Pallas kernels: none -> 3.3 us  [the longest x1 1.67 us: whole_shards(): pl.pallas_call(functools.partial(spread_body, emb_width), out_shape=jax.S...]
    unnamed x10 -> x2, local copies, waits for them, and re-layouts: 2.75 us -> 0.68 us
    convert_element_type x6 -> x0, other arithmetic: 1.84 us -> none  [the longest x2 0.92 us: shards(): row_sum.astype(jnp.bfloat16).reshape(col_count, piece_rows, channels)]
where the time goes in v1:
time: 32.8 us; the launch traced here: 32.4 us
  waiting for transfers between devices  13.2 us (40%)
  blocking collectives  7.34 us (22%)
  starting transfers between devices  7.3 us (22%)
  Pallas kernels  3.3 us (10%)
  local copies, waits for them, and re-layouts  1.3 us (4%)
    all_to_all x1, waiting for transfers between devices, whole_shards(): lax.all_to_all(sent, AXES, split_axis=0, concat_axis=0, tiled=True)  13.2 us
    all_to_all x1, blocking collectives, whole_shards(): lax.all_to_all(group_out.reshape(near, piece_rows, lanes), AXES, split_ax...  7.34 us
    all_to_all x1, starting transfers between devices, whole_shards(): lax.all_to_all(sent, AXES, split_axis=0, concat_axis=0, tiled=True)  7.3 us
    pallas_call x1, Pallas kernels, whole_shards(): pl.pallas_call(functools.partial(spread_body, emb_width), out_shape=jax.S...  1.67 us
    pallas_call x1, Pallas kernels, whole_shards(): pl.pallas_call(pack_body, out_shape=jax.ShapeDtypeStruct((peers, piece_ro...  1.63 us
    unnamed x2, local copies, waits for them, and re-layouts  0.68 us
  transfers between devices with their start and end apart: 1, of which 1 were waited for; matrix products, arithmetic and copies ran while one was open for 0% of the time, Pallas kernels for 0%

profile of v1, /device:TPU:0, one launch (start us, length us, event | category | flops | bytes accessed | tf_op | source)
XLA Modules:
  0.0 32.4 jit_solution(6651199257682249015)
XLA Ops:
  0.0 1.6 %shard_map.37 = bf16[32,16,384]{2,1,0:T(8,128)(2,1)} custom-call(bf16[16,256]{1,0:T(8,128)(2,1)} %emb_ref.1, bf16[16,1024]{1,0:T(8,128)(2,1)} %lab_ref.1), custom_call_target="tpu_custom_call" | custom-call | tf_op jit(solution)/shard_map/pallas_call | solution.py:204
  1.6 7.3 %all-to-all-start = ((bf16[32,16,384]{2,1,0:T(8,128)(2,1)}), bf16[32,16,384]{2,1,0:T(8,128)(2,1)S(1)}, u32[]{:S(2)}, u32[]{:S(2)}) async-start(bf16[32,16,384]{2,1,0:T(8,128)(2,1)} %shard_map.37), calls=%async_computation | async-start | bytes 786432 | tf_op jit(solution)/shard_map/all_to_all | solution.py:210
  9.0 13.2 %all-to-all-done = bf16[32,16,384]{2,1,0:T(8,128)(2,1)S(1)} async-done(((bf16[32,16,384]{2,1,0:T(8,128)(2,1)}), bf16[32,16,384]{2,1,0:T(8,128)(2,1)S(1)}, u32[]{:S(2)}, u32[]{:S(2)}) %all-to-all-start) | async-done | bytes 393248 | tf_op jit(solution)/shard_map/all_to_all | solution.py:210
  22.1 0.0 copy-start
  22.1 0.7 %copy-done = s32[2,2]{1,0:T(2,128)S(1)} copy-done((s32[2,2]{1,0:T(2,128)S(1)}, s32[2,2]{1,0:T(2,128)}, u32[]{:S(2)}) %copy-start) | copy-done | bytes 40
  22.8 1.7 %shard_map.38 = bf16[128,128]{1,0:T(8,128)(2,1)S(1)} custom-call(s32[2,2]{1,0:T(2,128)S(1)} %copy-done, s32[1]{0:T(128)} %bitcast.start_ref, bf16[512,384]{1,0:T(8,128)(2,1)S(1)} %bitcast.9), custom_call_target="tpu_custom_call" | custom-call | tf_op jit(solution)/shard_map/pallas_call | solution.py:213
  24.5 7.3 %all_to_all.10 = bf16[8,16,128]{2,1,0:T(8,128)(2,1)S(1)} all-to-all(bf16[8,16,128]{2,1,0:T(8,128)(2,1)S(1)} %bitcast.10), channel_id=1, replica_groups={{0,1,2,3,4,5,6,7},{8,9,10,11,12,13,14,15},{16,17,18,19,20,21,22,23},{24..., dimensions={0} | all-to-all | bytes 65536 | tf_op jit(solution)/shard_map/all_to_all | solution.py:221
  31.8 0.6 %copy_bitcast_fusion = bf16[16,1024]{1,0:T(8,128)(2,1)} fusion(bf16[8,16,128]{2,1,0:T(8,128)(2,1)S(1)} %all_to_all.10), kind=kLoop, calls=%fused_computation | loop fusion | bytes 65536 | tf_op jit(solution)/shard_map/reshape | solution.py:229
Async XLA Ops:
  1.6 20.5 %all-to-all-start = ((bf16[32,16,384]{2,1,0:T(8,128)(2,1)}), bf16[32,16,384]{2,1,0:T(8,128)(2,1)S(1)}, u32[]{:S(2)}, u32[]{:S(2)}) async-start(bf16[32,16,384]{2,1,0:T(8,128)(2,1)} %shard_map.37), calls=%async_computation | async-start | bytes 786432 | tf_op jit(solution)/shard_map/all_to_all | solution.py:210
  22.1 0.7 %copy-start = (s32[2,2]{1,0:T(2,128)S(1)}, s32[2,2]{1,0:T(2,128)}, u32[]{:S(2)}) copy-start(s32[2,2]{1,0:T(2,128)} %mask_ref.1) | copy-start | bytes 52

commit v2 on v1

--- a/solution.py
+++ b/solution.py
@@ -127,51 +127,72 @@
 
 
 AXES = ("row", "col")
-LANES = 128
+SHARE = 256
 WHOLE_KERNEL_BYTES = 4 * 1024 * 1024
 
 
-def pack_body(emb_ref, lab_ref, sent_ref):
+def pack_body(emb_hbm, lab_hbm, mask_hbm, sent_ref, kept_ref, emb_ref, lab_ref, sems):
+    copies = [
+        pltpu.make_async_copy(source, target, sems.at[k])
+        for k, (source, target) in enumerate(
+            ((emb_hbm, emb_ref), (lab_hbm, lab_ref), (mask_hbm, kept_ref))
+        )
+    ]
+    for copy in copies:
+        copy.start()
     peers, _, width = sent_ref.shape
     emb_width = emb_ref.shape[1]
-    lanes = width - emb_width
-    near = lab_ref.shape[1] // lanes
+    share = width - emb_width
+    team = lab_ref.shape[1] // share
+    copies[0].wait()
     unit_vecs = unit_rows(emb_ref[...])
     for peer in range(peers):
-        first = peer % near * lanes
         sent_ref[peer, :, :emb_width] = unit_vecs
-        sent_ref[peer, :, emb_width:] = lab_ref[:, first : first + lanes]
-
-
-def spread_body(emb_width, mask_ref, start_ref, all_ref, out_ref, kernel_ref):
-    images = all_ref.shape[0]
-    lanes = out_ref.shape[1]
-    blocks = images // BLOCK
+    copies[1].wait()
+    for peer in range(peers):
+        first = peer % team * share
+        sent_ref[peer, :, emb_width:] = lab_ref[:, first : first + share]
+    copies[2].wait()
+
+
+def spread_body(emb_width, start_ref, kept_ref, mine_ref, theirs_ref, out_ref, kernel_ref):
+    half = mine_ref.shape[0]
+    images = 2 * half
+    share = out_ref.shape[1]
+    segment = BLOCK // 2
+    blocks = half // segment
     sharpness = SHARPNESS * math.sqrt(emb_width)
-    for i in range(blocks):
-        rows = slice(i * BLOCK, (i + 1) * BLOCK)
-        for j in range(blocks):
-            cols = slice(j * BLOCK, (j + 1) * BLOCK)
+    halves = (mine_ref, theirs_ref)
+    for s in range(2):
+        for t in range(2):
             cosine = lax.dot_general(
-                all_ref[rows, :emb_width],
-                all_ref[cols, :emb_width],
+                halves[s][:, :emb_width],
+                halves[t][:, :emb_width],
                 (((1,), (1,)), ((), ())),
                 preferred_element_type=jnp.float32,
             )
             weights = jnp.exp(sharpness * cosine)
-            if i == j:
-                row_ids = lax.broadcasted_iota(jnp.int32, weights.shape, 0)
-                col_ids = lax.broadcasted_iota(jnp.int32, weights.shape, 1)
-                weights = jnp.where(row_ids == col_ids, 0.0, weights)
-            else:
-                weights = weights * mask_ref[min(i, j), max(i, j)].astype(jnp.float32)
-            kernel_ref[rows, cols] = weights.astype(jnp.bfloat16)
-    labels = all_ref[:, emb_width:].astype(jnp.float32)
+            for i in range(blocks):
+                for j in range(blocks):
+                    part = weights[
+                        i * segment : (i + 1) * segment, j * segment : (j + 1) * segment
+                    ]
+                    if i != j:
+                        low, high = min(i, j), max(i, j)
+                        part = part * kept_ref[low : low + 1, high : high + 1].astype(jnp.float32)
+                    elif s == t:
+                        row_ids = lax.broadcasted_iota(jnp.int32, part.shape, 0)
+                        col_ids = lax.broadcasted_iota(jnp.int32, part.shape, 1)
+                        part = jnp.where(row_ids == col_ids, 0.0, part)
+                    row = s * half + i * segment
+                    col = t * half + j * segment
+                    kernel_ref[row : row + segment, col : col + segment] = part.astype(jnp.bfloat16)
+    labels = jnp.concatenate([mine_ref[:, emb_width:], theirs_ref[:, emb_width:]], axis=0).astype(
+        jnp.float32
+    )
     weights = kernel_ref[...]
-    degree = jnp.dot(
-        weights, jnp.ones((images, lanes), jnp.bfloat16), preferred_element_type=jnp.float32
-    )
-    inv_root = lax.rsqrt(degree)
+    ones = jnp.ones((images, share), jnp.bfloat16)
+    inv_root = lax.rsqrt(jnp.dot(weights, ones, preferred_element_type=jnp.float32))
     current = labels
     for iteration in range(ITERS - 1):
         scaled = (inv_root * current).astype(jnp.bfloat16)
@@ -180,50 +201,64 @@
     scaled = (inv_root * current).astype(jnp.bfloat16)
     own_rows = pl.ds(pl.multiple_of(start_ref[0], 16), out_ref.shape[0])
     own_weights = kernel_ref[own_rows, :]
-    own_degree = jnp.dot(
-        own_weights, jnp.ones((images, lanes), jnp.bfloat16), preferred_element_type=jnp.float32
-    )
+    own_root = lax.rsqrt(jnp.dot(own_weights, ones, preferred_element_type=jnp.float32))
     spread = jnp.dot(own_weights, scaled, preferred_element_type=jnp.float32)
-    own_labels = all_ref[own_rows, emb_width:].astype(jnp.float32)
-    out_ref[...] = (
-        MIXING * lax.rsqrt(own_degree) * spread + (1.0 - MIXING) * own_labels
-    ).astype(jnp.bfloat16)
+    own_labels = mine_ref[own_rows, emb_width:].astype(jnp.float32)
+    out_ref[...] = (MIXING * own_root * spread + (1.0 - MIXING) * own_labels).astype(jnp.bfloat16)
 
 
 def whole_shards(embeddings, labels, tile_mask):
     piece_rows, emb_width = embeddings.shape
     channels = labels.shape[1]
-    lanes = LANES
-    near = channels // lanes
-    peers = lax.axis_size(AXES)
-    groups = [list(range(first, first + near)) for first in range(0, peers, near)]
-    images = peers * piece_rows
-    width = emb_width + lanes
+    team = channels // SHARE
+    devices = lax.axis_size(AXES)
+    peers = devices // 2
+    half = peers * piece_rows
+    width = emb_width + SHARE
+    same_core = [list(range(core, devices, 2)) for core in range(2)]
+    teams = [
+        list(range(first + core, first + 2 * team, 2))
+        for first in range(0, devices, 2 * team)
+        for core in range(2)
+    ]
     vmem = pl.BlockSpec(memory_space=pltpu.VMEM)
+    hbm = pl.BlockSpec(memory_space=pltpu.HBM)
     smem = pl.BlockSpec(memory_space=pltpu.SMEM)
-    sent = pl.pallas_call(
+    sent, kept = pl.pallas_call(
         pack_body,
-        out_shape=jax.ShapeDtypeStruct((peers, piece_rows, width), jnp.bfloat16),
-        in_specs=[vmem, vmem],
+        out_shape=(
+            jax.ShapeDtypeStruct((peers, piece_rows, width), jnp.bfloat16),
+            jax.ShapeDtypeStruct(tile_mask.shape, jnp.int32),
+        ),
+        in_specs=[hbm, hbm, hbm],
+        out_specs=(vmem, vmem),
+        scratch_shapes=[
+            pltpu.VMEM(embeddings.shape, embeddings.dtype),
+            pltpu.VMEM(labels.shape, labels.dtype),
+            pltpu.SemaphoreType.DMA((3,)),
+        ],
+        compiler_params=pltpu.CompilerParams(vmem_limit_bytes=8 * 1024 * 1024),
+    )(*(pltpu.with_memory_space_constraint(x, pltpu.HBM) for x in (embeddings, labels, tile_mask)))
+    mine = lax.all_to_all(
+        sent, AXES, split_axis=0, concat_axis=0, axis_index_groups=same_core, tiled=True
+    ).reshape(half, width)
+    theirs = lax.ppermute(mine, AXES, [(i, i ^ 1) for i in range(devices)])
+    team_rows = team * piece_rows
+    start = (lax.axis_index(AXES) // (2 * team) * team_rows).astype(jnp.int32).reshape(1)
+    team_out = pl.pallas_call(
+        functools.partial(spread_body, emb_width),
+        out_shape=jax.ShapeDtypeStruct((team_rows, SHARE), jnp.bfloat16),
+        in_specs=[smem, vmem, vmem, vmem],
         out_specs=vmem,
-    )(embeddings, labels)
-    arrived = lax.all_to_all(sent, AXES, split_axis=0, concat_axis=0, tiled=True)
-    group_rows = near * piece_rows
-    start = (lax.axis_index(AXES) // near * group_rows).astype(jnp.int32).reshape(1)
-    group_out = pl.pallas_call(
-        functools.partial(spread_body, emb_width),
-        out_shape=jax.ShapeDtypeStruct((group_rows, lanes), jnp.bfloat16),
-        in_specs=[smem, smem, vmem],
-        out_specs=vmem,
-        scratch_shapes=[pltpu.VMEM((images, images), jnp.bfloat16)],
+        scratch_shapes=[pltpu.VMEM((2 * half, 2 * half), jnp.bfloat16)],
         compiler_params=pltpu.CompilerParams(vmem_limit_bytes=32 * 1024 * 1024),
-    )(tile_mask, start, arrived.reshape(images, width))
+    )(start, kept, mine, theirs)
     pieces = lax.all_to_all(
-        group_out.reshape(near, piece_rows, lanes),
+        team_out.reshape(team, piece_rows, SHARE),
         AXES,
         split_axis=0,
         concat_axis=0,
-        axis_index_groups=groups,
+        axis_index_groups=teams,
         tiled=True,
     )
     return pieces.transpose(1, 0, 2).reshape(piece_rows, channels)
@@ -240,8 +275,9 @@
             images * images * 2 <= WHOLE_KERNEL_BYTES
             and images % (devices * 16) == 0
             and images % BLOCK == 0
-            and channels % LANES == 0
-            and devices % (channels // LANES) == 0
+            and BLOCK % (images // devices * 2) == 0
+            and channels % SHARE == 0
+            and devices % (channels // SHARE * 2) == 0
         )
         return jax.shard_map(
             whole_shards if whole else shards,

time: 32.8 us -> 29.5 us (0.90)
  blocking collectives: 7.34 us -> 25.1 us
  waiting for transfers between devices: 13.2 us -> 1.53 us
  starting transfers between devices: 7.3 us -> 0.01 us
  Pallas kernels: 3.3 us -> 1.96 us
  local copies, waits for them, and re-layouts: 1.3 us -> 0.62 us
    all_to_all x1 -> x2, blocking collectives: 7.34 us -> 25.1 us  [the longest x1 18 us: whole_shards(): lax.all_to_all(sent, AXES, split_axis=0, concat_axis=0, axis_index_groups...]
    all_to_all x1 -> x0, waiting for transfers between devices: 13.2 us -> none  [whole_shards(): lax.all_to_all(sent, AXES, split_axis=0, concat_axis=0, tiled=True)]
    all_to_all x1 -> x0, starting transfers between devices: 7.3 us -> none  [whole_shards(): lax.all_to_all(sent, AXES, split_axis=0, concat_axis=0, tiled=True)]
    ppermute x0 -> x1, waiting for transfers between devices: none -> 1.53 us  [whole_shards(): theirs = lax.ppermute(mine, AXES, [(i, i ^ 1) for i in range(devices)])]
    pallas_call x1, Pallas kernels: 1.63 us -> 0.83 us  [whole_shards(): pl.pallas_call(pack_body, out_shape=(jax.ShapeDtypeStruct((peers, piece_r...]
    unnamed x2 -> x0, local copies, waits for them, and re-layouts: 0.68 us -> none
    pallas_call x1, Pallas kernels: 1.67 us -> 1.13 us  [whole_shards(): pl.pallas_call(functools.partial(spread_body, emb_width), out_shape=jax.S...]
where the time goes in v2:
time: 29.5 us; the launch traced here: 29.2 us
  blocking collectives  25.1 us (85%)
  Pallas kernels  1.96 us (7%)
  waiting for transfers between devices  1.53 us (5%)
  local copies, waits for them, and re-layouts  0.62 us (2%)
    all_to_all x1, blocking collectives, whole_shards(): lax.all_to_all(sent, AXES, split_axis=0, concat_axis=0, axis_index_groups...  18 us
    all_to_all x1, blocking collectives, whole_shards(): lax.all_to_all(team_out.reshape(team, piece_rows, SHARE), AXES, split_axi...  7.11 us
    ppermute x1, waiting for transfers between devices, whole_shards(): theirs = lax.ppermute(mine, AXES, [(i, i ^ 1) for i in range(devices)])  1.53 us
    pallas_call x1, Pallas kernels, whole_shards(): pl.pallas_call(functools.partial(spread_body, emb_width), out_shape=jax.S...  1.13 us
    pallas_call x1, Pallas kernels, whole_shards(): pl.pallas_call(pack_body, out_shape=(jax.ShapeDtypeStruct((peers, piece_r...  0.83 us
    reshape x1, local copies, waits for them, and re-layouts, whole_shards(): return pieces.transpose(1, 0, 2).reshape(piece_rows, channels)  0.62 us
  transfers between devices with their start and end apart: 1, of which 1 were waited for; matrix products, arithmetic and copies ran while one was open for 0% of the time, Pallas kernels for 0%

profile of v2, /device:TPU:0, one launch (start us, length us, event | category | flops | bytes accessed | tf_op | source)
XLA Modules:
  0.0 29.2 jit_solution(7134942878764795373)
XLA Ops:
  0.0 0.8 %shard_map.37 = (bf16[16,16,512]{2,1,0:T(8,128)(2,1)S(1)}, s32[2,2]{1,0:T(2,128)S(1)}) custom-call(bf16[16,256]{1,0:T(8,128)(2,1)} %emb_hbm.1, bf16[16,1024]{1,0:T(8,128)(2,1)} %lab_hbm.1, s32[2,2]{1,0:T(2,128)} %mask_hbm.1), custom_call_target="tpu_custom_call" | custom-call | tf_op jit(solution)/shard_map/pallas_call | solution.py:227
  0.8 18.0 %all_to_all.10 = bf16[16,16,512]{2,1,0:T(8,128)(2,1)S(1)} all-to-all(bf16[16,16,512]{2,1,0:T(8,128)(2,1)S(1)} %get-tuple-element.8), channel_id=1, replica_groups={{0,2,4,6,8,10,12,14,16,18,20,22,24,26,28,30},{1,3,5,7,9,11,13,15,17,19,..., dimensions={0} | all-to-all | bytes 524288 | tf_op jit(solution)/shard_map/all_to_all | solution.py:242
  18.8 0.0 collective-permute-start
  18.8 1.5 %collective-permute-done.theirs_ref = bf16[256,512]{1,0:T(8,128)(2,1)S(1)} collective-permute-done((bf16[256,512]{1,0:T(8,128)(2,1)S(1)}, bf16[256,512]{1,0:T(8,128)(2,1)S(1)}, u32[]{:S(2)}, u32[]{:S(2)}) %collective-permute-start) | collective-permute-done | bytes 262176 | tf_op jit(solution)/shard_map/ppermute | solution.py:245
  20.4 1.1 %shard_map.38 = bf16[64,256]{1,0:T(8,128)(2,1)S(1)} custom-call(s32[1]{0:T(128)} %bitcast.start_ref, s32[2,2]{1,0:T(2,128)S(1)} %get-tuple-element.7.kept_ref, bf16[256,512]{1,0:T(8,128)(2,1)S(1)} %bitcast.7, bf16[256,512]{1,0:T(8,128)(2,1)S(1)} %collective-permute-done.theirs_ref), custom_call_target="tpu_custom_call" | custom-call | tf_op jit(solution)/shard_map/pallas_call | solution.py:248
  21.5 7.1 %all_to_all.11 = bf16[4,16,256]{2,1,0:T(8,128)(2,1)S(1)} all-to-all(bf16[4,16,256]{2,1,0:T(8,128)(2,1)S(1)} %bitcast.8), channel_id=1, replica_groups={{0,2,4,6},{1,3,5,7},{8,10,12,14},{9,11,13,15},{16,18,20,22},{17,19,21,2..., dimensions={0} | all-to-all | bytes 65536 | tf_op jit(solution)/shard_map/all_to_all | solution.py:256
  28.6 0.6 %copy.5 = bf16[4,2,8,256]{3,2,0,1:T(8,128)(2,1)} copy(bf16[4,2,8,256]{3,2,1,0:T(8,128)(2,1)S(1)} %bitcast.9) | data formatting | bytes 65536 | tf_op jit(solution)/shard_map/reshape | solution.py:264
Async XLA Ops:
  18.8 1.5 %collective-permute-start = (bf16[256,512]{1,0:T(8,128)(2,1)S(1)}, bf16[256,512]{1,0:T(8,128)(2,1)S(1)}, u32[]{:S(2)}, u32[]{:S(2)}) collective-permute-start(bf16[256,512]{1,0:T(8,128)(2,1)S(1)} %bitcast.6), channel_id=1, source_target_pairs={{0,1},{1,0},{2,3},{3,2},{4,5},{5,4},{6,7},{7,6},{8,9},{9,8},{10,11... | collective-permute-start | bytes 786440 | tf_op jit(solution)/shard_map/ppermute | solution.py:245

commit v3 on v2

--- a/solution.py
+++ b/solution.py
@@ -127,11 +127,26 @@
 
 
 AXES = ("row", "col")
-SHARE = 256
+CORES = 2
+SHARE = 128
 WHOLE_KERNEL_BYTES = 4 * 1024 * 1024
-
-
-def pack_body(emb_hbm, lab_hbm, mask_hbm, sent_ref, kept_ref, emb_ref, lab_ref, sems):
+ROOM = 8 * 1024 * 1024
+
+
+def chip_order(chips, team):
+    first = chips // 2 + chips // 4 - 1
+    return [first] + [chip for chip in range(chips) if chip != first]
+
+
+def team_order(team):
+    return list(range(team))[::-1]
+
+
+def crossed(chip, chips):
+    return int(chip >= chips // 2)
+
+
+def pack_body(order, emb_hbm, lab_hbm, mask_hbm, sent_ref, kept_ref, emb_ref, lab_ref, sems):
     copies = [
         pltpu.make_async_copy(source, target, sems.at[k])
         for k, (source, target) in enumerate(
@@ -150,61 +165,96 @@
         sent_ref[peer, :, :emb_width] = unit_vecs
     copies[1].wait()
     for peer in range(peers):
-        first = peer % team * share
+        first = order[peer] % team * share
         sent_ref[peer, :, emb_width:] = lab_ref[:, first : first + share]
     copies[2].wait()
 
 
-def spread_body(emb_width, start_ref, kept_ref, mine_ref, theirs_ref, out_ref, kernel_ref):
+def block_runs(order, piece):
+    runs = []
+    for place, chip in enumerate(order):
+        block = chip * CORES * piece // BLOCK
+        if runs and runs[-1][2] == block:
+            runs[-1][1] += piece
+        else:
+            runs.append([place * piece, (place + 1) * piece, block])
+    return runs
+
+
+def kernel_part(left, right, same, runs, kept_ref):
+    sharpness = SHARPNESS * math.sqrt(left.shape[1])
+    cosine = lax.dot_general(
+        left, right, (((1,), (1,)), ((), ())), preferred_element_type=jnp.float32
+    )
+    weights = jnp.exp(sharpness * cosine)
+    if same:
+        row_ids = lax.broadcasted_iota(jnp.int32, weights.shape, 0)
+        col_ids = lax.broadcasted_iota(jnp.int32, weights.shape, 1)
+        weights = jnp.where(row_ids == col_ids, 0.0, weights)
+    lines = []
+    for row, row_end, i in runs:
+        line = []
+        for col, col_end, j in runs:
+            part = weights[row:row_end, col:col_end]
+            if i != j:
+                low, high = min(i, j), max(i, j)
+                part = part * kept_ref[low : low + 1, high : high + 1].astype(jnp.float32)
+            line.append(part)
+        lines.append(jnp.concatenate(line, axis=1))
+    return jnp.concatenate(lines, axis=0).astype(jnp.bfloat16)
+
+
+def mine_body(runs, emb_width, kept_ref, mine_ref, part_ref):
+    mine = mine_ref[:, :emb_width]
+    part_ref[...] = kernel_part(mine, mine, True, runs, kept_ref)
+
+
+def spread_body(
+    emb_width, order, ranks, runs, run_ref, kept_ref, part_ref, mine_ref, theirs_ref, out_ref, kernel_ref
+):
+    chips = len(order)
+    team = len(ranks)
     half = mine_ref.shape[0]
-    images = 2 * half
+    piece = half // chips
     share = out_ref.shape[1]
-    segment = BLOCK // 2
-    blocks = half // segment
-    sharpness = SHARPNESS * math.sqrt(emb_width)
-    halves = (mine_ref, theirs_ref)
+    units = (mine_ref[:, :emb_width], theirs_ref[:, :emb_width])
+    ones = jnp.ones((half, share), jnp.bfloat16)
+    degrees = []
     for s in range(2):
+        degree = jnp.zeros((half, share), jnp.float32)
         for t in range(2):
-            cosine = lax.dot_general(
-                halves[s][:, :emb_width],
-                halves[t][:, :emb_width],
-                (((1,), (1,)), ((), ())),
-                preferred_element_type=jnp.float32,
-            )
-            weights = jnp.exp(sharpness * cosine)
-            for i in range(blocks):
-                for j in range(blocks):
-                    part = weights[
-                        i * segment : (i + 1) * segment, j * segment : (j + 1) * segment
-                    ]
-                    if i != j:
-                        low, high = min(i, j), max(i, j)
-                        part = part * kept_ref[low : low + 1, high : high + 1].astype(jnp.float32)
-                    elif s == t:
-                        row_ids = lax.broadcasted_iota(jnp.int32, part.shape, 0)
-                        col_ids = lax.broadcasted_iota(jnp.int32, part.shape, 1)
-                        part = jnp.where(row_ids == col_ids, 0.0, part)
-                    row = s * half + i * segment
-                    col = t * half + j * segment
-                    kernel_ref[row : row + segment, col : col + segment] = part.astype(jnp.bfloat16)
+            if s == 0 and t == 0:
+                weights = part_ref[...]
+            else:
+                weights = kernel_part(units[s], units[t], s == t, runs, kept_ref)
+            kernel_ref[s * half : (s + 1) * half, t * half : (t + 1) * half] = weights
+            degree = degree + jnp.dot(weights, ones, preferred_element_type=jnp.float32)
+        degrees.append(degree)
     labels = jnp.concatenate([mine_ref[:, emb_width:], theirs_ref[:, emb_width:]], axis=0).astype(
         jnp.float32
     )
     weights = kernel_ref[...]
-    ones = jnp.ones((images, share), jnp.bfloat16)
-    inv_root = lax.rsqrt(jnp.dot(weights, ones, preferred_element_type=jnp.float32))
+    inv_root = lax.rsqrt(jnp.concatenate(degrees, axis=0))
     current = labels
     for iteration in range(ITERS - 1):
         scaled = (inv_root * current).astype(jnp.bfloat16)
         spread = jnp.dot(weights, scaled, preferred_element_type=jnp.float32)
         current = MIXING * inv_root * spread + (1.0 - MIXING) * labels
     scaled = (inv_root * current).astype(jnp.bfloat16)
-    own_rows = pl.ds(pl.multiple_of(start_ref[0], 16), out_ref.shape[0])
-    own_weights = kernel_ref[own_rows, :]
+    own = []
+    for rank in ranks:
+        place = jnp.int32(0)
+        for run in range(chips // team):
+            place = jnp.where(run_ref[0] == run, order.index(run * team + rank), place)
+        own.append(pl.ds(pl.multiple_of(place * piece, 16), piece))
+    own_weights = jnp.concatenate([kernel_ref[rows, :] for rows in own], axis=0)
+    own_labels = jnp.concatenate([mine_ref[rows, emb_width:] for rows in own], axis=0)
+    ones = jnp.ones((2 * half, share), jnp.bfloat16)
     own_root = lax.rsqrt(jnp.dot(own_weights, ones, preferred_element_type=jnp.float32))
     spread = jnp.dot(own_weights, scaled, preferred_element_type=jnp.float32)
-    own_labels = mine_ref[own_rows, emb_width:].astype(jnp.float32)
-    out_ref[...] = (MIXING * own_root * spread + (1.0 - MIXING) * own_labels).astype(jnp.bfloat16)
+    out_ref[...] = (
+        MIXING * own_root * spread + (1.0 - MIXING) * own_labels.astype(jnp.float32)
+    ).astype(jnp.bfloat16)
 
 
 def whole_shards(embeddings, labels, tile_mask):
@@ -212,22 +262,28 @@
     channels = labels.shape[1]
     team = channels // SHARE
     devices = lax.axis_size(AXES)
-    peers = devices // 2
-    half = peers * piece_rows
+    chips = devices // CORES
+    half = chips * piece_rows
     width = emb_width + SHARE
-    same_core = [list(range(core, devices, 2)) for core in range(2)]
+    order = chip_order(chips, team)
+    ranks = team_order(team)
+    runs = block_runs(order, piece_rows)
+    sides = [
+        [chip * CORES + (side ^ crossed(chip, chips)) for chip in range(chips)]
+        for side in range(CORES)
+    ]
+    gathered = [[side[chip] for chip in order] for side in sides]
     teams = [
-        list(range(first + core, first + 2 * team, 2))
-        for first in range(0, devices, 2 * team)
-        for core in range(2)
+        [side[first + rank] for rank in ranks] for first in range(0, chips, team) for side in sides
     ]
     vmem = pl.BlockSpec(memory_space=pltpu.VMEM)
     hbm = pl.BlockSpec(memory_space=pltpu.HBM)
     smem = pl.BlockSpec(memory_space=pltpu.SMEM)
+    room = pltpu.CompilerParams(vmem_limit_bytes=ROOM)
     sent, kept = pl.pallas_call(
-        pack_body,
+        functools.partial(pack_body, order),
         out_shape=(
-            jax.ShapeDtypeStruct((peers, piece_rows, width), jnp.bfloat16),
+            jax.ShapeDtypeStruct((chips, piece_rows, width), jnp.bfloat16),
             jax.ShapeDtypeStruct(tile_mask.shape, jnp.int32),
         ),
         in_specs=[hbm, hbm, hbm],
@@ -237,22 +293,33 @@
             pltpu.VMEM(labels.shape, labels.dtype),
             pltpu.SemaphoreType.DMA((3,)),
         ],
-        compiler_params=pltpu.CompilerParams(vmem_limit_bytes=8 * 1024 * 1024),
+        compiler_params=room,
     )(*(pltpu.with_memory_space_constraint(x, pltpu.HBM) for x in (embeddings, labels, tile_mask)))
     mine = lax.all_to_all(
-        sent, AXES, split_axis=0, concat_axis=0, axis_index_groups=same_core, tiled=True
+        sent, AXES, split_axis=0, concat_axis=0, axis_index_groups=gathered, tiled=True
     ).reshape(half, width)
     theirs = lax.ppermute(mine, AXES, [(i, i ^ 1) for i in range(devices)])
-    team_rows = team * piece_rows
-    start = (lax.axis_index(AXES) // (2 * team) * team_rows).astype(jnp.int32).reshape(1)
+    part = pl.pallas_call(
+        functools.partial(mine_body, runs, emb_width),
+        out_shape=jax.ShapeDtypeStruct((half, half), jnp.bfloat16),
+        in_specs=[vmem, vmem],
+        out_specs=vmem,
+        compiler_params=room,
+        cost_estimate=pl.CostEstimate(
+            flops=2 * half * half * emb_width,
+            bytes_accessed=2 * half * (half + emb_width),
+            transcendentals=half * half,
+        ),
+    )(kept, mine)
+    run = (lax.axis_index(AXES) // (CORES * team)).astype(jnp.int32).reshape(1)
     team_out = pl.pallas_call(
-        functools.partial(spread_body, emb_width),
-        out_shape=jax.ShapeDtypeStruct((team_rows, SHARE), jnp.bfloat16),
-        in_specs=[smem, vmem, vmem, vmem],
+        functools.partial(spread_body, emb_width, order, ranks, runs),
+        out_shape=jax.ShapeDtypeStruct((team * piece_rows, SHARE), jnp.bfloat16),
+        in_specs=[smem, vmem, vmem, vmem, vmem],
         out_specs=vmem,
         scratch_shapes=[pltpu.VMEM((2 * half, 2 * half), jnp.bfloat16)],
-        compiler_params=pltpu.CompilerParams(vmem_limit_bytes=32 * 1024 * 1024),
-    )(start, kept, mine, theirs)
+        compiler_params=room,
+    )(run, kept, part, mine, theirs)
     pieces = lax.all_to_all(
         team_out.reshape(team, piece_rows, SHARE),
         AXES,
@@ -261,7 +328,8 @@
         axis_index_groups=teams,
         tiled=True,
     )
-    return pieces.transpose(1, 0, 2).reshape(piece_rows, channels)
+    rows = jnp.stack([pieces[ranks.index(rank)] for rank in range(team)], axis=1)
+    return rows.reshape(piece_rows, channels)
 
 
 def solution(mesh):
@@ -274,10 +342,9 @@
         whole = (
             images * images * 2 <= WHOLE_KERNEL_BYTES
             and images % (devices * 16) == 0
-            and images % BLOCK == 0
-            and BLOCK % (images // devices * 2) == 0
+            and BLOCK % (images // devices * CORES) == 0
             and channels % SHARE == 0
-            and devices % (channels // SHARE * 2) == 0
+            and devices % (channels // SHARE * CORES) == 0
         )
         return jax.shard_map(
             whole_shards if whole else shards,

time: 29.5 us -> 24.8 us (0.84)
  blocking collectives: 25.1 us -> 19.7 us
  starting transfers between devices: 0.01 us -> 1.15 us
  waiting for transfers between devices: 1.53 us -> 0.82 us
    all_to_all x1, blocking collectives: 18 us -> 12.3 us  [whole_shards(): lax.all_to_all(sent, AXES, split_axis=0, concat_axis=0, axis_index_groups...]
    ppermute x1, starting transfers between devices: 0.01 us -> 1.15 us  [whole_shards(): theirs = lax.ppermute(mine, AXES, [(i, i ^ 1) for i in range(devices)])]
    ppermute x1, waiting for transfers between devices: 1.53 us -> 0.82 us  [whole_shards(): theirs = lax.ppermute(mine, AXES, [(i, i ^ 1) for i in range(devices)])]
    pallas_call x2 -> x3, Pallas kernels: 1.96 us -> 2.15 us  [the longest x1 1.07 us: whole_shards(): pl.pallas_call(functools.partial(spread_body, emb_width, order, ranks, ru...]
  transfers between devices with their start and end apart: 1 -> 1, of which waited for: 1 -> 1; matrix products, arithmetic and copies ran while one was open for 0% -> 0% of each run, Pallas kernels for 0% -> 1%
where the time goes in v3:
time: 24.8 us; the launch traced here: 24.5 us
  blocking collectives  19.7 us (79%)
  Pallas kernels  2.15 us (9%)
  starting transfers between devices  1.15 us (5%)
  waiting for transfers between devices  0.82 us (3%)
  local copies, waits for them, and re-layouts  0.68 us (3%)
    all_to_all x1, blocking collectives, whole_shards(): lax.all_to_all(sent, AXES, split_axis=0, concat_axis=0, axis_index_groups...  12.3 us
    all_to_all x1, blocking collectives, whole_shards(): lax.all_to_all(team_out.reshape(team, piece_rows, SHARE), AXES, split_axi...  7.39 us
    ppermute x1, starting transfers between devices, whole_shards(): theirs = lax.ppermute(mine, AXES, [(i, i ^ 1) for i in range(devices)])  1.15 us
    pallas_call x1, Pallas kernels, whole_shards(): pl.pallas_call(functools.partial(spread_body, emb_width, order, ranks, ru...  1.07 us
    pallas_call x1, Pallas kernels, whole_shards(): pl.pallas_call(functools.partial(pack_body, order), out_shape=(jax.ShapeD...  0.83 us
    ppermute x1, waiting for transfers between devices, whole_shards(): theirs = lax.ppermute(mine, AXES, [(i, i ^ 1) for i in range(devices)])  0.82 us
    reshape x1, local copies, waits for them, and re-layouts, whole_shards(): return rows.reshape(piece_rows, channels)  0.62 us
  transfers between devices with their start and end apart: 1, of which 1 were waited for; matrix products, arithmetic and copies ran while one was open for 0% of the time, Pallas kernels for 1%

profile of v3, /device:TPU:0, one launch (start us, length us, event | category | flops | bytes accessed | tf_op | source)
XLA Modules:
  0.0 24.5 jit_solution(5456827356788967720)
XLA Ops:
  0.0 0.8 %shard_map.37 = (bf16[16,16,384]{2,1,0:T(8,128)(2,1)S(1)}, s32[2,2]{1,0:T(2,128)S(1)}) custom-call(bf16[16,256]{1,0:T(8,128)(2,1)} %emb_hbm.1, bf16[16,1024]{1,0:T(8,128)(2,1)} %lab_hbm.1, s32[2,2]{1,0:T(2,128)} %mask_hbm.1), custom_call_target="tpu_custom_call" | custom-call | tf_op jit(solution)/shard_map/pallas_call | solution.py:283
  0.8 12.3 %all_to_all.10 = bf16[16,16,384]{2,1,0:T(8,128)(2,1)S(1)} all-to-all(bf16[16,16,384]{2,1,0:T(8,128)(2,1)S(1)} %get-tuple-element.8), channel_id=1, replica_groups={{23,0,2,4,6,8,10,12,14,17,19,21,25,27,29,31},{22,1,3,5,7,9,11,13,15,16,..., dimensions={0} | all-to-all | bytes 393216 | tf_op jit(solution)/shard_map/all_to_all | solution.py:298
  13.2 1.2 %collective-permute-start = (bf16[256,384]{1,0:T(8,128)(2,1)S(1)}, bf16[256,384]{1,0:T(8,128)(2,1)S(1)}, u32[]{:S(2)}, u32[]{:S(2)}) collective-permute-start(bf16[256,384]{1,0:T(8,128)(2,1)S(1)} %bitcast.40), channel_id=1, source_target_pairs={{0,1},{1,0},{2,3},{3,2},{4,5},{5,4},{6,7},{7,6},{8,9},{9,8},{10,11... | collective-permute-start | bytes 589832 | tf_op jit(solution)/shard_map/ppermute | solution.py:301
  14.3 0.2 %shard_map.38.part_ref = bf16[256,256]{1,0:T(8,128)(2,1)S(1)} custom-call(s32[2,2]{1,0:T(2,128)S(1)} %get-tuple-element.7.kept_ref, bf16[256,384]{1,0:T(8,128)(2,1)S(1)} %bitcast.41), custom_call_target="tpu_custom_call" | custom-call | flops 33554432 | bytes 262144 | tf_op jit(solution)/shard_map/pallas_call | solution.py:302
  14.6 0.8 %collective-permute-done.theirs_ref = bf16[256,384]{1,0:T(8,128)(2,1)S(1)} collective-permute-done((bf16[256,384]{1,0:T(8,128)(2,1)S(1)}, bf16[256,384]{1,0:T(8,128)(2,1)S(1)}, u32[]{:S(2)}, u32[]{:S(2)}) %collective-permute-start) | collective-permute-done | bytes 196640 | tf_op jit(solution)/shard_map/ppermute | solution.py:301
  15.4 1.1 %shard_map.39 = bf16[128,128]{1,0:T(8,128)(2,1)S(1)} custom-call(s32[1]{0:T(128)} %bitcast.run_ref, s32[2,2]{1,0:T(2,128)S(1)} %get-tuple-element.7.kept_ref, bf16[256,256]{1,0:T(8,128)(2,1)S(1)} %shard_map.38.part_ref, bf16[256,384]{1,0:T(8,128)(2,1)S(1)} %bitcast.42, bf16[256,384]{1,0:T(8,128)(2,1)S(1)} %collective-permute-done.theirs_ref), custom_call_target="tpu_custom_call" | custom-call | tf_op jit(solution)/shard_map/pallas_call | solution.py:315
  16.5 7.4 %all_to_all.11 = bf16[8,16,128]{2,1,0:T(8,128)(2,1)S(1)} all-to-all(bf16[8,16,128]{2,1,0:T(8,128)(2,1)S(1)} %bitcast.43), channel_id=1, replica_groups={{14,12,10,8,6,4,2,0},{15,13,11,9,7,5,3,1},{31,29,27,25,23,21,19,17},{30..., dimensions={0} | all-to-all | bytes 65536 | tf_op jit(solution)/shard_map/all_to_all | solution.py:323
  23.9 0.6 %copy_bitcast_fusion = bf16[16,1024]{1,0:T(8,128)(2,1)} fusion(bf16[16,8,128]{2,0,1:T(8,128)(2,1)S(1)} %constant_dynamic-update-slice_fusion), kind=kLoop, calls=%fused_computation | loop fusion | bytes 65536 | tf_op jit(solution)/shard_map/reshape | solution.py:332
  (8 shorter events, 0.1 us)
Async XLA Ops:
  13.2 2.2 %collective-permute-start = (bf16[256,384]{1,0:T(8,128)(2,1)S(1)}, bf16[256,384]{1,0:T(8,128)(2,1)S(1)}, u32[]{:S(2)}, u32[]{:S(2)}) collective-permute-start(bf16[256,384]{1,0:T(8,128)(2,1)S(1)} %bitcast.40), channel_id=1, source_target_pairs={{0,1},{1,0},{2,3},{3,2},{4,5},{5,4},{6,7},{7,6},{8,9},{9,8},{10,11... | collective-permute-start | bytes 589832 | tf_op jit(solution)/shard_map/ppermute | solution.py:301

commit v4 on v3

--- a/solution.py
+++ b/solution.py
@@ -133,17 +133,17 @@
 ROOM = 8 * 1024 * 1024
 
 
-def chip_order(chips, team):
+def chip_order(chips):
     first = chips // 2 + chips // 4 - 1
     return [first] + [chip for chip in range(chips) if chip != first]
 
 
 def team_order(team):
-    return list(range(team))[::-1]
+    return [team - 1] + list(range(team - 1))
 
 
 def crossed(chip, chips):
-    return int(chip >= chips // 2)
+    return int(0 < chip < chips // 2)
 
 
 def pack_body(order, emb_hbm, lab_hbm, mask_hbm, sent_ref, kept_ref, emb_ref, lab_ref, sems):
@@ -204,13 +204,19 @@
     return jnp.concatenate(lines, axis=0).astype(jnp.bfloat16)
 
 
-def mine_body(runs, emb_width, kept_ref, mine_ref, part_ref):
+def row_sums(weights):
+    return jnp.sum(weights.astype(jnp.float32), axis=1, keepdims=True)
+
+
+def mine_body(runs, emb_width, kept_ref, mine_ref, part_ref, sums_ref):
     mine = mine_ref[:, :emb_width]
-    part_ref[...] = kernel_part(mine, mine, True, runs, kept_ref)
+    weights = kernel_part(mine, mine, True, runs, kept_ref)
+    part_ref[...] = weights
+    sums_ref[...] = jnp.broadcast_to(row_sums(weights), sums_ref.shape)
 
 
 def spread_body(
-    emb_width, order, ranks, runs, run_ref, kept_ref, part_ref, mine_ref, theirs_ref, out_ref, kernel_ref
+    emb_width, order, ranks, runs, run_ref, kept_ref, part_ref, sums_ref, mine_ref, theirs_ref, out_ref, kernel_ref, root_ref
 ):
     chips = len(order)
     team = len(ranks)
@@ -218,23 +224,19 @@
     piece = half // chips
     share = out_ref.shape[1]
     units = (mine_ref[:, :emb_width], theirs_ref[:, :emb_width])
-    ones = jnp.ones((half, share), jnp.bfloat16)
-    degrees = []
-    for s in range(2):
-        degree = jnp.zeros((half, share), jnp.float32)
-        for t in range(2):
-            if s == 0 and t == 0:
-                weights = part_ref[...]
-            else:
-                weights = kernel_part(units[s], units[t], s == t, runs, kept_ref)
-            kernel_ref[s * half : (s + 1) * half, t * half : (t + 1) * half] = weights
-            degree = degree + jnp.dot(weights, ones, preferred_element_type=jnp.float32)
-        degrees.append(degree)
+    kernel_ref[:half, :half] = part_ref[...]
+    degrees = [sums_ref[...], jnp.zeros((half, 1), jnp.float32)]
+    for s, t in ((0, 1), (1, 0), (1, 1)):
+        weights = kernel_part(units[s], units[t], s == t, runs, kept_ref)
+        kernel_ref[s * half : (s + 1) * half, t * half : (t + 1) * half] = weights
+        degrees[s] = degrees[s] + row_sums(weights)
+    degrees[1] = jnp.broadcast_to(degrees[1], (half, share))
     labels = jnp.concatenate([mine_ref[:, emb_width:], theirs_ref[:, emb_width:]], axis=0).astype(
         jnp.float32
     )
     weights = kernel_ref[...]
     inv_root = lax.rsqrt(jnp.concatenate(degrees, axis=0))
+    root_ref[...] = inv_root[:half]
     current = labels
     for iteration in range(ITERS - 1):
         scaled = (inv_root * current).astype(jnp.bfloat16)
@@ -249,12 +251,17 @@
         own.append(pl.ds(pl.multiple_of(place * piece, 16), piece))
     own_weights = jnp.concatenate([kernel_ref[rows, :] for rows in own], axis=0)
     own_labels = jnp.concatenate([mine_ref[rows, emb_width:] for rows in own], axis=0)
-    ones = jnp.ones((2 * half, share), jnp.bfloat16)
-    own_root = lax.rsqrt(jnp.dot(own_weights, ones, preferred_element_type=jnp.float32))
+    own_root = jnp.concatenate([root_ref[rows, :] for rows in own], axis=0)
     spread = jnp.dot(own_weights, scaled, preferred_element_type=jnp.float32)
     out_ref[...] = (
         MIXING * own_root * spread + (1.0 - MIXING) * own_labels.astype(jnp.float32)
     ).astype(jnp.bfloat16)
+
+
+def place_body(ranks, pieces_ref, out_ref):
+    share = pieces_ref.shape[2]
+    for place, rank in enumerate(ranks):
+        out_ref[:, rank * share : (rank + 1) * share] = pieces_ref[place]
 
 
 def whole_shards(embeddings, labels, tile_mask):
@@ -265,7 +272,7 @@
     chips = devices // CORES
     half = chips * piece_rows
     width = emb_width + SHARE
-    order = chip_order(chips, team)
+    order = chip_order(chips)
     ranks = team_order(team)
     runs = block_runs(order, piece_rows)
     sides = [
@@ -299,11 +306,14 @@
         sent, AXES, split_axis=0, concat_axis=0, axis_index_groups=gathered, tiled=True
     ).reshape(half, width)
     theirs = lax.ppermute(mine, AXES, [(i, i ^ 1) for i in range(devices)])
-    part = pl.pallas_call(
+    part, sums = pl.pallas_call(
         functools.partial(mine_body, runs, emb_width),
-        out_shape=jax.ShapeDtypeStruct((half, half), jnp.bfloat16),
+        out_shape=(
+            jax.ShapeDtypeStruct((half, half), jnp.bfloat16),
+            jax.ShapeDtypeStruct((half, SHARE), jnp.float32),
+        ),
         in_specs=[vmem, vmem],
-        out_specs=vmem,
+        out_specs=(vmem, vmem),
         compiler_params=room,
         cost_estimate=pl.CostEstimate(
             flops=2 * half * half * emb_width,
@@ -315,11 +325,14 @@
     team_out = pl.pallas_call(
         functools.partial(spread_body, emb_width, order, ranks, runs),
         out_shape=jax.ShapeDtypeStruct((team * piece_rows, SHARE), jnp.bfloat16),
-        in_specs=[smem, vmem, vmem, vmem, vmem],
+        in_specs=[smem, vmem, vmem, vmem, vmem, vmem],
         out_specs=vmem,
-        scratch_shapes=[pltpu.VMEM((2 * half, 2 * half), jnp.bfloat16)],
+        scratch_shapes=[
+            pltpu.VMEM((2 * half, 2 * half), jnp.bfloat16),
+            pltpu.VMEM((half, SHARE), jnp.float32),
+        ],
         compiler_params=room,
-    )(run, kept, part, mine, theirs)
+    )(run, kept, part, sums, mine, theirs)
     pieces = lax.all_to_all(
         team_out.reshape(team, piece_rows, SHARE),
         AXES,
@@ -328,8 +341,13 @@
         axis_index_groups=teams,
         tiled=True,
     )
-    rows = jnp.stack([pieces[ranks.index(rank)] for rank in range(team)], axis=1)
-    return rows.reshape(piece_rows, channels)
+    return pl.pallas_call(
+        functools.partial(place_body, ranks),
+        out_shape=jax.ShapeDtypeStruct((piece_rows, channels), jnp.bfloat16),
+        in_specs=[vmem],
+        out_specs=vmem,
+        compiler_params=room,
+    )(pieces)
 
 
 def solution(mesh):

time: 24.8 us -> 24.3 us (0.980)
  starting transfers between devices: 1.15 us -> 0.01 us
  local copies, waits for them, and re-layouts: 0.68 us -> 0 us
  Pallas kernels: 2.15 us -> 2.77 us
  blocking collectives: 19.7 us -> 20.2 us
  waiting for transfers between devices: 0.82 us -> 1.09 us
    all_to_all x1, blocking collectives: 12.3 us -> 13.7 us  [whole_shards(): lax.all_to_all(sent, AXES, split_axis=0, concat_axis=0, axis_index_groups...]
    ppermute x1, starting transfers between devices: 1.15 us -> 0.01 us  [whole_shards(): theirs = lax.ppermute(mine, AXES, [(i, i ^ 1) for i in range(devices)])]
    all_to_all x1, blocking collectives: 7.39 us -> 6.52 us  [whole_shards(): lax.all_to_all(team_out.reshape(team, piece_rows, SHARE), AXES, split_axi...]
    pallas_call x1 -> x2, Pallas kernels: 0.25 us -> 0.96 us  [the longest x1 0.62 us: whole_shards(): pl.pallas_call(functools.partial(place_body, ranks), out_shape=jax.ShapeD...]
    reshape x1 -> x0, local copies, waits for them, and re-layouts: 0.62 us -> none  [whole_shards(): return rows.reshape(piece_rows, channels)]
    ppermute x1, waiting for transfers between devices: 0.82 us -> 1.09 us  [whole_shards(): theirs = lax.ppermute(mine, AXES, [(i, i ^ 1) for i in range(devices)])]
where the time goes in v4:
time: 24.3 us; the launch traced here: 24.1 us
  blocking collectives  20.2 us (83%)
  Pallas kernels  2.77 us (11%)
  waiting for transfers between devices  1.09 us (4%)
    all_to_all x1, blocking collectives, whole_shards(): lax.all_to_all(sent, AXES, split_axis=0, concat_axis=0, axis_index_groups...  13.7 us
    all_to_all x1, blocking collectives, whole_shards(): lax.all_to_all(team_out.reshape(team, piece_rows, SHARE), AXES, split_axi...  6.52 us
    ppermute x1, waiting for transfers between devices, whole_shards(): theirs = lax.ppermute(mine, AXES, [(i, i ^ 1) for i in range(devices)])  1.09 us
    pallas_call x1, Pallas kernels, whole_shards(): pl.pallas_call(functools.partial(spread_body, emb_width, order, ranks, ru...  0.97 us
    pallas_call x1, Pallas kernels, whole_shards(): pl.pallas_call(functools.partial(pack_body, order), out_shape=(jax.ShapeD...  0.83 us
    pallas_call x1, Pallas kernels, whole_shards(): pl.pallas_call(functools.partial(place_body, ranks), out_shape=jax.ShapeD...  0.62 us
  transfers between devices with their start and end apart: 1, of which 1 were waited for; matrix products, arithmetic and copies ran while one was open for 0% of the time, Pallas kernels for 1%

profile of v4, /device:TPU:0, one launch (start us, length us, event | category | flops | bytes accessed | tf_op | source)
XLA Modules:
  0.0 24.1 jit_solution(7202983041314010087)
XLA Ops:
  0.0 0.8 %shard_map.37 = (bf16[16,16,384]{2,1,0:T(8,128)(2,1)S(1)}, s32[2,2]{1,0:T(2,128)S(1)}) custom-call(bf16[16,256]{1,0:T(8,128)(2,1)} %emb_hbm.1, bf16[16,1024]{1,0:T(8,128)(2,1)} %lab_hbm.1, s32[2,2]{1,0:T(2,128)} %mask_hbm.1), custom_call_target="tpu_custom_call" | custom-call | tf_op jit(solution)/shard_map/pallas_call | solution.py:290
  0.8 13.7 %all_to_all.10 = bf16[16,16,384]{2,1,0:T(8,128)(2,1)S(1)} all-to-all(bf16[16,16,384]{2,1,0:T(8,128)(2,1)S(1)} %get-tuple-element.10), channel_id=1, replica_groups={{22,0,3,5,7,9,11,13,15,16,18,20,24,26,28,30},{23,1,2,4,6,8,10,12,14,17,..., dimensions={0} | all-to-all | bytes 393216 | tf_op jit(solution)/shard_map/all_to_all | solution.py:305
  14.5 0.0 collective-permute-start
  14.5 0.3 %shard_map.38 = (bf16[256,256]{1,0:T(8,128)(2,1)S(1)}, f32[256,128]{1,0:T(8,128)S(1)}) custom-call(s32[2,2]{1,0:T(2,128)S(1)} %get-tuple-element.9.kept_ref, bf16[256,384]{1,0:T(8,128)(2,1)S(1)} %bitcast.4), custom_call_target="tpu_custom_call" | custom-call | flops 33554432 | bytes 262144 | tf_op jit(solution)/shard_map/pallas_call | solution.py:309
  14.8 1.1 %collective-permute-done.theirs_ref = bf16[256,384]{1,0:T(8,128)(2,1)S(1)} collective-permute-done((bf16[256,384]{1,0:T(8,128)(2,1)S(1)}, bf16[256,384]{1,0:T(8,128)(2,1)S(1)}, u32[]{:S(2)}, u32[]{:S(2)}) %collective-permute-start) | collective-permute-done | bytes 196640 | tf_op jit(solution)/shard_map/ppermute | solution.py:308
  15.9 1.0 %shard_map.39 = bf16[128,128]{1,0:T(8,128)(2,1)S(1)} custom-call(s32[1]{0:T(128)} %bitcast.run_ref, s32[2,2]{1,0:T(2,128)S(1)} %get-tuple-element.9.kept_ref, bf16[256,256]{1,0:T(8,128)(2,1)S(1)} %get-tuple-element.11.part_ref, f32[256,128]{1,0:T(8,128)S(1)} %get-tuple-element.12.sums_ref, bf16[256,384]{1,0:T(8,128)(2,1)S(1)} %bitcast.5, ...), custom_call_target="tpu_custom_call" | custom-call | tf_op jit(solution)/shard_map/pallas_call | solution.py:325
  16.9 6.5 %all_to_all.11.pieces_ref = bf16[8,16,128]{2,1,0:T(8,128)(2,1)S(1)} all-to-all(bf16[8,16,128]{2,1,0:T(8,128)(2,1)S(1)} %bitcast.6), channel_id=1, replica_groups={{15,0,3,5,7,9,11,13},{14,1,2,4,6,8,10,12},{30,16,18,20,22,24,26,28},{31..., dimensions={0} | all-to-all | bytes 65536 | tf_op jit(solution)/shard_map/all_to_all | solution.py:336
  23.4 0.6 %shard_map.40 = bf16[16,1024]{1,0:T(8,128)(2,1)} custom-call(bf16[8,16,128]{2,1,0:T(8,128)(2,1)S(1)} %all_to_all.11.pieces_ref), custom_call_target="tpu_custom_call" | custom-call | tf_op jit(solution)/shard_map/pallas_call | solution.py:344
Async XLA Ops:
  14.5 1.4 %collective-permute-start = (bf16[256,384]{1,0:T(8,128)(2,1)S(1)}, bf16[256,384]{1,0:T(8,128)(2,1)S(1)}, u32[]{:S(2)}, u32[]{:S(2)}) collective-permute-start(bf16[256,384]{1,0:T(8,128)(2,1)S(1)} %bitcast.3), channel_id=1, source_target_pairs={{0,1},{1,0},{2,3},{3,2},{4,5},{5,4},{6,7},{7,6},{8,9},{9,8},{10,11... | collective-permute-start | bytes 589832 | tf_op jit(solution)/shard_map/ppermute | solution.py:308

commit v5 on v4

--- a/solution.py
+++ b/solution.py
@@ -142,8 +142,12 @@
     return [team - 1] + list(range(team - 1))
 
 
-def crossed(chip, chips):
-    return int(0 < chip < chips // 2)
+def gather_flip(chip, chips):
+    return 1 * (chip >= chips // 2)
+
+
+def team_flip(chip, chips):
+    return 1 * (chip > 0) * (chip < chips // 2)
 
 
 def pack_body(order, emb_hbm, lab_hbm, mask_hbm, sent_ref, kept_ref, emb_ref, lab_ref, sems):
@@ -216,8 +220,9 @@
 
 
 def spread_body(
-    emb_width, order, ranks, runs, run_ref, kept_ref, part_ref, sums_ref, mine_ref, theirs_ref, out_ref, kernel_ref, root_ref
+    emb_width, order, ranks, runs, rank_ref, kept_ref, part_ref, sums_ref, mine_ref, theirs_ref, out_ref, *scratch
 ):
+    kernel_ref, root_ref, label_ref = scratch
     chips = len(order)
     team = len(ranks)
     half = mine_ref.shape[0]
@@ -231,26 +236,30 @@
         kernel_ref[s * half : (s + 1) * half, t * half : (t + 1) * half] = weights
         degrees[s] = degrees[s] + row_sums(weights)
     degrees[1] = jnp.broadcast_to(degrees[1], (half, share))
-    labels = jnp.concatenate([mine_ref[:, emb_width:], theirs_ref[:, emb_width:]], axis=0).astype(
-        jnp.float32
-    )
+    label_ref[:half] = mine_ref[:, emb_width:]
+    label_ref[half:] = theirs_ref[:, emb_width:]
+    labels = label_ref[...].astype(jnp.float32)
     weights = kernel_ref[...]
     inv_root = lax.rsqrt(jnp.concatenate(degrees, axis=0))
-    root_ref[...] = inv_root[:half]
+    root_ref[...] = inv_root
     current = labels
     for iteration in range(ITERS - 1):
         scaled = (inv_root * current).astype(jnp.bfloat16)
         spread = jnp.dot(weights, scaled, preferred_element_type=jnp.float32)
         current = MIXING * inv_root * spread + (1.0 - MIXING) * labels
     scaled = (inv_root * current).astype(jnp.bfloat16)
+    chip, core = rank_ref[0] // CORES, rank_ref[0] % CORES
+    gather_side = core ^ gather_flip(chip, chips)
+    team_side = core ^ team_flip(chip, chips)
     own = []
     for rank in ranks:
-        place = jnp.int32(0)
-        for run in range(chips // team):
-            place = jnp.where(run_ref[0] == run, order.index(run * team + rank), place)
-        own.append(pl.ds(pl.multiple_of(place * piece, 16), piece))
+        target = chip // team * team + rank
+        side = team_side ^ team_flip(target, chips) ^ gather_flip(target, chips)
+        place = jnp.where(target == order[0], 0, target + 1 * (target < order[0]))
+        row = place * piece + half * (side ^ gather_side)
+        own.append(pl.ds(pl.multiple_of(row, 16), piece))
     own_weights = jnp.concatenate([kernel_ref[rows, :] for rows in own], axis=0)
-    own_labels = jnp.concatenate([mine_ref[rows, emb_width:] for rows in own], axis=0)
+    own_labels = jnp.concatenate([label_ref[rows, :] for rows in own], axis=0)
     own_root = jnp.concatenate([root_ref[rows, :] for rows in own], axis=0)
     spread = jnp.dot(own_weights, scaled, preferred_element_type=jnp.float32)
     out_ref[...] = (
@@ -275,13 +284,14 @@
     order = chip_order(chips)
     ranks = team_order(team)
     runs = block_runs(order, piece_rows)
-    sides = [
-        [chip * CORES + (side ^ crossed(chip, chips)) for chip in range(chips)]
+    gathered = [
+        [chip * CORES + (side ^ gather_flip(chip, chips)) for chip in order]
         for side in range(CORES)
     ]
-    gathered = [[side[chip] for chip in order] for side in sides]
     teams = [
-        [side[first + rank] for rank in ranks] for first in range(0, chips, team) for side in sides
+        [chip * CORES + (side ^ team_flip(chip, chips)) for chip in (first + rank for rank in ranks)]
+        for first in range(0, chips, team)
+        for side in range(CORES)
     ]
     vmem = pl.BlockSpec(memory_space=pltpu.VMEM)
     hbm = pl.BlockSpec(memory_space=pltpu.HBM)
@@ -321,7 +331,7 @@
             transcendentals=half * half,
         ),
     )(kept, mine)
-    run = (lax.axis_index(AXES) // (CORES * team)).astype(jnp.int32).reshape(1)
+    rank = lax.axis_index(AXES).astype(jnp.int32).reshape(1)
     team_out = pl.pallas_call(
         functools.partial(spread_body, emb_width, order, ranks, runs),
         out_shape=jax.ShapeDtypeStruct((team * piece_rows, SHARE), jnp.bfloat16),
@@ -329,10 +339,11 @@
         out_specs=vmem,
         scratch_shapes=[
             pltpu.VMEM((2 * half, 2 * half), jnp.bfloat16),
-            pltpu.VMEM((half, SHARE), jnp.float32),
+            pltpu.VMEM((2 * half, SHARE), jnp.float32),
+            pltpu.VMEM((2 * half, SHARE), jnp.bfloat16),
         ],
         compiler_params=room,
-    )(run, kept, part, sums, mine, theirs)
+    )(rank, kept, part, sums, mine, theirs)
     pieces = lax.all_to_all(
         team_out.reshape(team, piece_rows, SHARE),
         AXES,

time: 24.3 us -> 24 us (0.988)
  starting transfers between devices: 0.01 us -> 1.15 us
  blocking collectives: 20.2 us -> 19.1 us
  waiting for transfers between devices: 1.09 us -> 0.72 us
    all_to_all x1, blocking collectives: 13.7 us -> 12.3 us  [whole_shards(): lax.all_to_all(sent, AXES, split_axis=0, concat_axis=0, axis_index_groups...]
    ppermute x1, starting transfers between devices: 0.01 us -> 1.15 us  [whole_shards(): theirs = lax.ppermute(mine, AXES, [(i, i ^ 1) for i in range(devices)])]
    ppermute x1, waiting for transfers between devices: 1.09 us -> 0.72 us  [whole_shards(): theirs = lax.ppermute(mine, AXES, [(i, i ^ 1) for i in range(devices)])]
where the time goes in v5:
time: 24 us; the launch traced here: 23.8 us
  blocking collectives  19.1 us (80%)
  Pallas kernels  2.82 us (12%)
  starting transfers between devices  1.15 us (5%)
  waiting for transfers between devices  0.72 us (3%)
    all_to_all x1, blocking collectives, whole_shards(): lax.all_to_all(sent, AXES, split_axis=0, concat_axis=0, axis_index_groups...  12.3 us
    all_to_all x1, blocking collectives, whole_shards(): lax.all_to_all(team_out.reshape(team, piece_rows, SHARE), AXES, split_axi...  6.73 us
    ppermute x1, starting transfers between devices, whole_shards(): theirs = lax.ppermute(mine, AXES, [(i, i ^ 1) for i in range(devices)])  1.15 us
    pallas_call x1, Pallas kernels, whole_shards(): pl.pallas_call(functools.partial(spread_body, emb_width, order, ranks, ru...  1.03 us
    pallas_call x1, Pallas kernels, whole_shards(): pl.pallas_call(functools.partial(pack_body, order), out_shape=(jax.ShapeD...  0.83 us
    ppermute x1, waiting for transfers between devices, whole_shards(): theirs = lax.ppermute(mine, AXES, [(i, i ^ 1) for i in range(devices)])  0.72 us
    pallas_call x1, Pallas kernels, whole_shards(): pl.pallas_call(functools.partial(place_body, ranks), out_shape=jax.ShapeD...  0.62 us
  transfers between devices with their start and end apart: 1, of which 1 were waited for; matrix products, arithmetic and copies ran while one was open for 0% of the time, Pallas kernels for 1%

profile of v5, /device:TPU:0, one launch (start us, length us, event | category | flops | bytes accessed | tf_op | source)
XLA Modules:
  0.0 23.8 jit_solution(4912886243854629245)
XLA Ops:
  0.0 0.8 %shard_map.37 = (bf16[16,16,384]{2,1,0:T(8,128)(2,1)S(1)}, s32[2,2]{1,0:T(2,128)S(1)}) custom-call(bf16[16,256]{1,0:T(8,128)(2,1)} %emb_hbm.1, bf16[16,1024]{1,0:T(8,128)(2,1)} %lab_hbm.1, s32[2,2]{1,0:T(2,128)} %mask_hbm.1), custom_call_target="tpu_custom_call" | custom-call | tf_op jit(solution)/shard_map/pallas_call | solution.py:300
  0.8 12.3 %all_to_all.10 = bf16[16,16,384]{2,1,0:T(8,128)(2,1)S(1)} all-to-all(bf16[16,16,384]{2,1,0:T(8,128)(2,1)S(1)} %get-tuple-element.10), channel_id=1, replica_groups={{23,0,2,4,6,8,10,12,14,17,19,21,25,27,29,31},{22,1,3,5,7,9,11,13,15,16,..., dimensions={0} | all-to-all | bytes 393216 | tf_op jit(solution)/shard_map/all_to_all | solution.py:315
  13.2 1.2 %collective-permute-start = (bf16[256,384]{1,0:T(8,128)(2,1)S(1)}, bf16[256,384]{1,0:T(8,128)(2,1)S(1)}, u32[]{:S(2)}, u32[]{:S(2)}) collective-permute-start(bf16[256,384]{1,0:T(8,128)(2,1)S(1)} %bitcast.3), channel_id=1, source_target_pairs={{0,1},{1,0},{2,3},{3,2},{4,5},{5,4},{6,7},{7,6},{8,9},{9,8},{10,11... | collective-permute-start | bytes 589832 | tf_op jit(solution)/shard_map/ppermute | solution.py:318
  14.3 0.3 %shard_map.38 = (bf16[256,256]{1,0:T(8,128)(2,1)S(1)}, f32[256,128]{1,0:T(8,128)S(1)}) custom-call(s32[2,2]{1,0:T(2,128)S(1)} %get-tuple-element.9.kept_ref, bf16[256,384]{1,0:T(8,128)(2,1)S(1)} %bitcast.4), custom_call_target="tpu_custom_call" | custom-call | flops 33554432 | bytes 262144 | tf_op jit(solution)/shard_map/pallas_call | solution.py:319
  14.7 0.7 %collective-permute-done.theirs_ref = bf16[256,384]{1,0:T(8,128)(2,1)S(1)} collective-permute-done((bf16[256,384]{1,0:T(8,128)(2,1)S(1)}, bf16[256,384]{1,0:T(8,128)(2,1)S(1)}, u32[]{:S(2)}, u32[]{:S(2)}) %collective-permute-start) | collective-permute-done | bytes 196640 | tf_op jit(solution)/shard_map/ppermute | solution.py:318
  15.4 1.0 %shard_map.39 = bf16[128,128]{1,0:T(8,128)(2,1)S(1)} custom-call(s32[1]{0:T(128)} %bitcast.rank_ref, s32[2,2]{1,0:T(2,128)S(1)} %get-tuple-element.9.kept_ref, bf16[256,256]{1,0:T(8,128)(2,1)S(1)} %get-tuple-element.11.part_ref, f32[256,128]{1,0:T(8,128)S(1)} %get-tuple-element.12.sums_ref, bf16[256,384]{1,0:T(8,128)(2,1)S(1)} %bitcast.5, ...), custom_call_target="tpu_custom_call" | custom-call | tf_op jit(solution)/shard_map/pallas_call | solution.py:335
  16.4 6.7 %all_to_all.11.pieces_ref = bf16[8,16,128]{2,1,0:T(8,128)(2,1)S(1)} all-to-all(bf16[8,16,128]{2,1,0:T(8,128)(2,1)S(1)} %bitcast.6), channel_id=1, replica_groups={{15,0,3,5,7,9,11,13},{14,1,2,4,6,8,10,12},{30,16,18,20,22,24,26,28},{31..., dimensions={0} | all-to-all | bytes 65536 | tf_op jit(solution)/shard_map/all_to_all | solution.py:347
  23.1 0.6 %shard_map.40 = bf16[16,1024]{1,0:T(8,128)(2,1)} custom-call(bf16[8,16,128]{2,1,0:T(8,128)(2,1)S(1)} %all_to_all.11.pieces_ref), custom_call_target="tpu_custom_call" | custom-call | tf_op jit(solution)/shard_map/pallas_call | solution.py:355
Async XLA Ops:
  13.2 2.2 %collective-permute-start = (bf16[256,384]{1,0:T(8,128)(2,1)S(1)}, bf16[256,384]{1,0:T(8,128)(2,1)S(1)}, u32[]{:S(2)}, u32[]{:S(2)}) collective-permute-start(bf16[256,384]{1,0:T(8,128)(2,1)S(1)} %bitcast.3), channel_id=1, source_target_pairs={{0,1},{1,0},{2,3},{3,2},{4,5},{5,4},{6,7},{7,6},{8,9},{9,8},{10,11... | collective-permute-start | bytes 589832 | tf_op jit(solution)/shard_map/ppermute | solution.py:318

commit v6 on v5

--- a/solution.py
+++ b/solution.py
@@ -231,22 +231,27 @@
     units = (mine_ref[:, :emb_width], theirs_ref[:, :emb_width])
     kernel_ref[:half, :half] = part_ref[...]
     degrees = [sums_ref[...], jnp.zeros((half, 1), jnp.float32)]
-    for s, t in ((0, 1), (1, 0), (1, 1)):
-        weights = kernel_part(units[s], units[t], s == t, runs, kept_ref)
-        kernel_ref[s * half : (s + 1) * half, t * half : (t + 1) * half] = weights
-        degrees[s] = degrees[s] + row_sums(weights)
-    degrees[1] = jnp.broadcast_to(degrees[1], (half, share))
-    label_ref[:half] = mine_ref[:, emb_width:]
-    label_ref[half:] = theirs_ref[:, emb_width:]
-    labels = label_ref[...].astype(jnp.float32)
+    across = kernel_part(units[0], units[1], False, runs, kept_ref)
+    theirs = kernel_part(units[1], units[1], True, runs, kept_ref)
+    back = across.T
+    kernel_ref[:half, half:] = across
+    kernel_ref[half:, :half] = back
+    kernel_ref[half:, half:] = theirs
+    degrees[0] = degrees[0] + row_sums(across)
+    degrees[1] = jnp.broadcast_to(row_sums(back) + row_sums(theirs), (half, share))
+    labels = jnp.concatenate([mine_ref[:, emb_width:], theirs_ref[:, emb_width:]], axis=0).astype(
+        jnp.float32
+    )
     weights = kernel_ref[...]
     inv_root = lax.rsqrt(jnp.concatenate(degrees, axis=0))
-    root_ref[...] = inv_root
+    root_ref[...] = MIXING * inv_root
+    kept_part = (1.0 - MIXING) * labels
+    label_ref[...] = kept_part
     current = labels
     for iteration in range(ITERS - 1):
         scaled = (inv_root * current).astype(jnp.bfloat16)
         spread = jnp.dot(weights, scaled, preferred_element_type=jnp.float32)
-        current = MIXING * inv_root * spread + (1.0 - MIXING) * labels
+        current = MIXING * inv_root * spread + kept_part
     scaled = (inv_root * current).astype(jnp.bfloat16)
     chip, core = rank_ref[0] // CORES, rank_ref[0] % CORES
     gather_side = core ^ gather_flip(chip, chips)
@@ -262,9 +267,7 @@
     own_labels = jnp.concatenate([label_ref[rows, :] for rows in own], axis=0)
     own_root = jnp.concatenate([root_ref[rows, :] for rows in own], axis=0)
     spread = jnp.dot(own_weights, scaled, preferred_element_type=jnp.float32)
-    out_ref[...] = (
-        MIXING * own_root * spread + (1.0 - MIXING) * own_labels.astype(jnp.float32)
-    ).astype(jnp.bfloat16)
+    out_ref[...] = (own_root * spread + own_labels).astype(jnp.bfloat16)
 
 
 def place_body(ranks, pieces_ref, out_ref):
@@ -340,7 +343,7 @@
         scratch_shapes=[
             pltpu.VMEM((2 * half, 2 * half), jnp.bfloat16),
             pltpu.VMEM((2 * half, SHARE), jnp.float32),
-            pltpu.VMEM((2 * half, SHARE), jnp.bfloat16),
+            pltpu.VMEM((2 * half, SHARE), jnp.float32),
         ],
         compiler_params=room,
     )(rank, kept, part, sums, mine, theirs)

time: 24 us -> 23.9 us (level)
  no operation moved by 1% of the time
where the time goes in v6:
time: 23.9 us; the launch traced here: 23.7 us
  blocking collectives  19.1 us (80%)
  Pallas kernels  2.71 us (11%)
  starting transfers between devices  1.15 us (5%)
  waiting for transfers between devices  0.72 us (3%)
    all_to_all x1, blocking collectives, whole_shards(): lax.all_to_all(sent, AXES, split_axis=0, concat_axis=0, axis_index_groups...  12.3 us
    all_to_all x1, blocking collectives, whole_shards(): lax.all_to_all(team_out.reshape(team, piece_rows, SHARE), AXES, split_axi...  6.73 us
    ppermute x1, starting transfers between devices, whole_shards(): theirs = lax.ppermute(mine, AXES, [(i, i ^ 1) for i in range(devices)])  1.15 us
    pallas_call x1, Pallas kernels, whole_shards(): pl.pallas_call(functools.partial(spread_body, emb_width, order, ranks, ru...  0.91 us
    pallas_call x1, Pallas kernels, whole_shards(): pl.pallas_call(functools.partial(pack_body, order), out_shape=(jax.ShapeD...  0.83 us
    ppermute x1, waiting for transfers between devices, whole_shards(): theirs = lax.ppermute(mine, AXES, [(i, i ^ 1) for i in range(devices)])  0.72 us
    pallas_call x1, Pallas kernels, whole_shards(): pl.pallas_call(functools.partial(place_body, ranks), out_shape=jax.ShapeD...  0.62 us
  transfers between devices with their start and end apart: 1, of which 1 were waited for; matrix products, arithmetic and copies ran while one was open for 0% of the time, Pallas kernels for 1%

profile of v6, /device:TPU:0, one launch (start us, length us, event | category | flops | bytes accessed | tf_op | source)
XLA Modules:
  0.0 23.7 jit_solution(16898237484784519265)
XLA Ops:
  0.0 0.8 %shard_map.37 = (bf16[16,16,384]{2,1,0:T(8,128)(2,1)S(1)}, s32[2,2]{1,0:T(2,128)S(1)}) custom-call(bf16[16,256]{1,0:T(8,128)(2,1)} %emb_hbm.1, bf16[16,1024]{1,0:T(8,128)(2,1)} %lab_hbm.1, s32[2,2]{1,0:T(2,128)} %mask_hbm.1), custom_call_target="tpu_custom_call" | custom-call | tf_op jit(solution)/shard_map/pallas_call | solution.py:303
  0.8 12.3 %all_to_all.10 = bf16[16,16,384]{2,1,0:T(8,128)(2,1)S(1)} all-to-all(bf16[16,16,384]{2,1,0:T(8,128)(2,1)S(1)} %get-tuple-element.10), channel_id=1, replica_groups={{23,0,2,4,6,8,10,12,14,17,19,21,25,27,29,31},{22,1,3,5,7,9,11,13,15,16,..., dimensions={0} | all-to-all | bytes 393216 | tf_op jit(solution)/shard_map/all_to_all | solution.py:318
  13.2 1.2 %collective-permute-start = (bf16[256,384]{1,0:T(8,128)(2,1)S(1)}, bf16[256,384]{1,0:T(8,128)(2,1)S(1)}, u32[]{:S(2)}, u32[]{:S(2)}) collective-permute-start(bf16[256,384]{1,0:T(8,128)(2,1)S(1)} %bitcast.3), channel_id=1, source_target_pairs={{0,1},{1,0},{2,3},{3,2},{4,5},{5,4},{6,7},{7,6},{8,9},{9,8},{10,11... | collective-permute-start | bytes 589832 | tf_op jit(solution)/shard_map/ppermute | solution.py:321
  14.3 0.3 %shard_map.38 = (bf16[256,256]{1,0:T(8,128)(2,1)S(1)}, f32[256,128]{1,0:T(8,128)S(1)}) custom-call(s32[2,2]{1,0:T(2,128)S(1)} %get-tuple-element.9.kept_ref, bf16[256,384]{1,0:T(8,128)(2,1)S(1)} %bitcast.4), custom_call_target="tpu_custom_call" | custom-call | flops 33554432 | bytes 262144 | tf_op jit(solution)/shard_map/pallas_call | solution.py:322
  14.7 0.7 %collective-permute-done.theirs_ref = bf16[256,384]{1,0:T(8,128)(2,1)S(1)} collective-permute-done((bf16[256,384]{1,0:T(8,128)(2,1)S(1)}, bf16[256,384]{1,0:T(8,128)(2,1)S(1)}, u32[]{:S(2)}, u32[]{:S(2)}) %collective-permute-start) | collective-permute-done | bytes 196640 | tf_op jit(solution)/shard_map/ppermute | solution.py:321
  15.4 0.9 %shard_map.39 = bf16[128,128]{1,0:T(8,128)(2,1)S(1)} custom-call(s32[1]{0:T(128)} %bitcast.rank_ref, s32[2,2]{1,0:T(2,128)S(1)} %get-tuple-element.9.kept_ref, bf16[256,256]{1,0:T(8,128)(2,1)S(1)} %get-tuple-element.11.part_ref, f32[256,128]{1,0:T(8,128)S(1)} %get-tuple-element.12.sums_ref, bf16[256,384]{1,0:T(8,128)(2,1)S(1)} %bitcast.5, ...), custom_call_target="tpu_custom_call" | custom-call | tf_op jit(solution)/shard_map/pallas_call | solution.py:338
  16.3 6.7 %all_to_all.11.pieces_ref = bf16[8,16,128]{2,1,0:T(8,128)(2,1)S(1)} all-to-all(bf16[8,16,128]{2,1,0:T(8,128)(2,1)S(1)} %bitcast.6), channel_id=1, replica_groups={{15,0,3,5,7,9,11,13},{14,1,2,4,6,8,10,12},{30,16,18,20,22,24,26,28},{31..., dimensions={0} | all-to-all | bytes 65536 | tf_op jit(solution)/shard_map/all_to_all | solution.py:350
  23.0 0.6 %shard_map.40 = bf16[16,1024]{1,0:T(8,128)(2,1)} custom-call(bf16[8,16,128]{2,1,0:T(8,128)(2,1)S(1)} %all_to_all.11.pieces_ref), custom_call_target="tpu_custom_call" | custom-call | tf_op jit(solution)/shard_map/pallas_call | solution.py:358
Async XLA Ops:
  13.2 2.2 %collective-permute-start = (bf16[256,384]{1,0:T(8,128)(2,1)S(1)}, bf16[256,384]{1,0:T(8,128)(2,1)S(1)}, u32[]{:S(2)}, u32[]{:S(2)}) collective-permute-start(bf16[256,384]{1,0:T(8,128)(2,1)S(1)} %bitcast.3), channel_id=1, source_target_pairs={{0,1},{1,0},{2,3},{3,2},{4,5},{5,4},{6,7},{7,6},{8,9},{9,8},{10,11... | collective-permute-start | bytes 589832 | tf_op jit(solution)/shard_map/ppermute | solution.py:321

commit v7 on v6

--- a/solution.py
+++ b/solution.py
@@ -128,7 +128,8 @@
 
 AXES = ("row", "col")
 CORES = 2
-SHARE = 128
+SHARE = 512
+LANES = 128
 WHOLE_KERNEL_BYTES = 4 * 1024 * 1024
 ROOM = 8 * 1024 * 1024
 
@@ -138,16 +139,8 @@
     return [first] + [chip for chip in range(chips) if chip != first]
 
 
-def team_order(team):
-    return [team - 1] + list(range(team - 1))
-
-
 def gather_flip(chip, chips):
     return 1 * (chip >= chips // 2)
-
-
-def team_flip(chip, chips):
-    return 1 * (chip > 0) * (chip < chips // 2)
 
 
 def pack_body(order, emb_hbm, lab_hbm, mask_hbm, sent_ref, kept_ref, emb_ref, lab_ref, sems):
@@ -219,61 +212,82 @@
     sums_ref[...] = jnp.broadcast_to(row_sums(weights), sums_ref.shape)
 
 
-def spread_body(
-    emb_width, order, ranks, runs, rank_ref, kept_ref, part_ref, sums_ref, mine_ref, theirs_ref, out_ref, *scratch
+def own_place(rank, order, step, piece):
+    chips = len(order)
+    chip, core = rank // CORES, rank % CORES
+    target = chip ^ step
+    place = jnp.where(target == order[0], 0, target + 1 * (target < order[0]))
+    other = gather_flip(chip, chips) ^ gather_flip(target, chips) ^ min(step, 1)
+    return pl.multiple_of(place * piece, 16), other
+
+
+def whole_body(
+    order, team, runs, emb_width, rank_ref, kept_ref, part_ref, sums_ref, mine_ref, start_ref, *rest
 ):
-    kernel_ref, root_ref, label_ref = scratch
-    chips = len(order)
-    team = len(ranks)
+    steps_ref, root_ref, kernel_ref = rest
     half = mine_ref.shape[0]
-    piece = half // chips
-    share = out_ref.shape[1]
-    units = (mine_ref[:, :emb_width], theirs_ref[:, :emb_width])
+    piece = half // len(order)
+    units = (mine_ref[:, :emb_width], start_ref[:, :emb_width])
     kernel_ref[:half, :half] = part_ref[...]
-    degrees = [sums_ref[...], jnp.zeros((half, 1), jnp.float32)]
     across = kernel_part(units[0], units[1], False, runs, kept_ref)
     theirs = kernel_part(units[1], units[1], True, runs, kept_ref)
     back = across.T
     kernel_ref[:half, half:] = across
     kernel_ref[half:, :half] = back
     kernel_ref[half:, half:] = theirs
-    degrees[0] = degrees[0] + row_sums(across)
-    degrees[1] = jnp.broadcast_to(row_sums(back) + row_sums(theirs), (half, share))
-    labels = jnp.concatenate([mine_ref[:, emb_width:], theirs_ref[:, emb_width:]], axis=0).astype(
-        jnp.float32
+    degree = sums_ref[...] + row_sums(across)
+    roots = lax.rsqrt(
+        jnp.concatenate(
+            [degree, jnp.broadcast_to(row_sums(back) + row_sums(theirs), degree.shape)], axis=0
+        )
     )
-    weights = kernel_ref[...]
-    inv_root = lax.rsqrt(jnp.concatenate(degrees, axis=0))
-    root_ref[...] = MIXING * inv_root
-    kept_part = (1.0 - MIXING) * labels
-    label_ref[...] = kept_part
-    current = labels
+    root_ref[...] = roots
+    weights = kernel_ref[...].astype(jnp.float32)
+    shares = jnp.concatenate([roots * roots] * (2 * half // LANES), axis=1)
+    passed = (shares * weights).astype(jnp.bfloat16)
+    own = []
+    for step in range(team):
+        place, other = own_place(rank_ref[0], order, step, piece)
+        own.append(kernel_ref[pl.ds(pl.multiple_of(place + half * other, 16), piece), :])
+    first = MIXING * jnp.concatenate(own, axis=0).astype(jnp.float32)
+    steps = first
     for iteration in range(ITERS - 1):
-        scaled = (inv_root * current).astype(jnp.bfloat16)
-        spread = jnp.dot(weights, scaled, preferred_element_type=jnp.float32)
-        current = MIXING * inv_root * spread + kept_part
-    scaled = (inv_root * current).astype(jnp.bfloat16)
-    chip, core = rank_ref[0] // CORES, rank_ref[0] % CORES
-    gather_side = core ^ gather_flip(chip, chips)
-    team_side = core ^ team_flip(chip, chips)
-    own = []
-    for rank in ranks:
-        target = chip // team * team + rank
-        side = team_side ^ team_flip(target, chips) ^ gather_flip(target, chips)
-        place = jnp.where(target == order[0], 0, target + 1 * (target < order[0]))
-        row = place * piece + half * (side ^ gather_side)
-        own.append(pl.ds(pl.multiple_of(row, 16), piece))
-    own_weights = jnp.concatenate([kernel_ref[rows, :] for rows in own], axis=0)
-    own_labels = jnp.concatenate([label_ref[rows, :] for rows in own], axis=0)
-    own_root = jnp.concatenate([root_ref[rows, :] for rows in own], axis=0)
-    spread = jnp.dot(own_weights, scaled, preferred_element_type=jnp.float32)
-    out_ref[...] = (own_root * spread + own_labels).astype(jnp.bfloat16)
-
-
-def place_body(ranks, pieces_ref, out_ref):
-    share = pieces_ref.shape[2]
-    for place, rank in enumerate(ranks):
-        out_ref[:, rank * share : (rank + 1) * share] = pieces_ref[place]
+        steps = MIXING * jnp.dot(
+            steps.astype(jnp.bfloat16), passed, preferred_element_type=jnp.float32
+        ) + (1.0 - MIXING) * first
+    steps_ref[...] = steps.astype(jnp.bfloat16)
+
+
+def spread_body(emb_width, order, rank_ref, steps_ref, root_ref, mine_ref, start_ref, end_ref, *out_refs):
+    half = mine_ref.shape[0]
+    share = mine_ref.shape[1] - emb_width
+    piece = half // len(order)
+    theirs = jnp.concatenate([start_ref[:, emb_width:], end_ref[...]], axis=1)
+    labels = jnp.concatenate([mine_ref[:, emb_width:], theirs], axis=0).astype(jnp.float32)
+    inv_root = jnp.concatenate([root_ref[...]] * (share // LANES), axis=1)
+    scaled = (inv_root * labels).astype(jnp.bfloat16)
+    spread = jnp.dot(steps_ref[...], scaled, preferred_element_type=jnp.float32)
+    for step, out_ref in enumerate(out_refs):
+        place, other = own_place(rank_ref[0], order, step, piece)
+        rows = pl.ds(place, piece)
+        root = root_ref[pl.ds(pl.multiple_of(place + half * other, 16), piece), :]
+        root = jnp.concatenate([root] * (share // LANES), axis=1)
+        theirs = jnp.concatenate([start_ref[rows, emb_width:], end_ref[rows, :]], axis=1)
+        own = jnp.where(
+            other == 0, mine_ref[rows, emb_width:].astype(jnp.float32), theirs.astype(jnp.float32)
+        )
+        out_ref[...] = (
+            root * spread[step * piece : (step + 1) * piece] + (1.0 - MIXING) * own
+        ).astype(jnp.bfloat16)
+
+
+def place_body(rank_ref, *refs):
+    pieces, out_ref = refs[:-1], refs[-1]
+    share = pieces[0].shape[1]
+    chip = rank_ref[0] // CORES
+    for step, piece_ref in enumerate(pieces):
+        first = pl.multiple_of((chip ^ step) % len(pieces) * share, LANES)
+        out_ref[:, pl.ds(first, share)] = piece_ref[...]
 
 
 def whole_shards(embeddings, labels, tile_mask):
@@ -285,15 +299,9 @@
     half = chips * piece_rows
     width = emb_width + SHARE
     order = chip_order(chips)
-    ranks = team_order(team)
     runs = block_runs(order, piece_rows)
     gathered = [
         [chip * CORES + (side ^ gather_flip(chip, chips)) for chip in order]
-        for side in range(CORES)
-    ]
-    teams = [
-        [chip * CORES + (side ^ team_flip(chip, chips)) for chip in (first + rank for rank in ranks)]
-        for first in range(0, chips, team)
         for side in range(CORES)
     ]
     vmem = pl.BlockSpec(memory_space=pltpu.VMEM)
@@ -318,12 +326,15 @@
     mine = lax.all_to_all(
         sent, AXES, split_axis=0, concat_axis=0, axis_index_groups=gathered, tiled=True
     ).reshape(half, width)
-    theirs = lax.ppermute(mine, AXES, [(i, i ^ 1) for i in range(devices)])
+    swap = [(i, i ^ 1) for i in range(devices)]
+    middle = width // 2
+    their_start = lax.ppermute(mine[:, :middle], AXES, swap)
+    their_end = lax.ppermute(mine[:, middle:], AXES, swap)
     part, sums = pl.pallas_call(
         functools.partial(mine_body, runs, emb_width),
         out_shape=(
             jax.ShapeDtypeStruct((half, half), jnp.bfloat16),
-            jax.ShapeDtypeStruct((half, SHARE), jnp.float32),
+            jax.ShapeDtypeStruct((half, LANES), jnp.float32),
         ),
         in_specs=[vmem, vmem],
         out_specs=(vmem, vmem),
@@ -335,33 +346,41 @@
         ),
     )(kept, mine)
     rank = lax.axis_index(AXES).astype(jnp.int32).reshape(1)
-    team_out = pl.pallas_call(
-        functools.partial(spread_body, emb_width, order, ranks, runs),
-        out_shape=jax.ShapeDtypeStruct((team * piece_rows, SHARE), jnp.bfloat16),
-        in_specs=[smem, vmem, vmem, vmem, vmem, vmem],
-        out_specs=vmem,
-        scratch_shapes=[
-            pltpu.VMEM((2 * half, 2 * half), jnp.bfloat16),
-            pltpu.VMEM((2 * half, SHARE), jnp.float32),
-            pltpu.VMEM((2 * half, SHARE), jnp.float32),
-        ],
+    steps, root = pl.pallas_call(
+        functools.partial(whole_body, order, team, runs, emb_width),
+        out_shape=(
+            jax.ShapeDtypeStruct((team * piece_rows, 2 * half), jnp.bfloat16),
+            jax.ShapeDtypeStruct((2 * half, LANES), jnp.float32),
+        ),
+        in_specs=[smem] + [vmem] * 5,
+        out_specs=(vmem, vmem),
+        scratch_shapes=[pltpu.VMEM((2 * half, 2 * half), jnp.bfloat16)],
         compiler_params=room,
-    )(rank, kept, part, sums, mine, theirs)
-    pieces = lax.all_to_all(
-        team_out.reshape(team, piece_rows, SHARE),
-        AXES,
-        split_axis=0,
-        concat_axis=0,
-        axis_index_groups=teams,
-        tiled=True,
-    )
+        cost_estimate=pl.CostEstimate(
+            flops=4 * half * half * emb_width,
+            bytes_accessed=8 * half * half,
+            transcendentals=2 * half * half,
+        ),
+    )(rank, kept, part, sums, mine, their_start)
+    piece = jax.ShapeDtypeStruct((piece_rows, SHARE), jnp.bfloat16)
+    kept_piece, *sent_pieces = pl.pallas_call(
+        functools.partial(spread_body, emb_width, order),
+        out_shape=(piece,) * team,
+        in_specs=[smem] + [vmem] * 5,
+        out_specs=(vmem,) * team,
+        compiler_params=room,
+    )(rank, steps, root, mine, their_start, their_end)
+    pieces = [kept_piece] + [
+        lax.ppermute(sent_piece, AXES, [(i, i ^ (CORES * step + 1)) for i in range(devices)])
+        for step, sent_piece in enumerate(sent_pieces, 1)
+    ]
     return pl.pallas_call(
-        functools.partial(place_body, ranks),
+        place_body,
         out_shape=jax.ShapeDtypeStruct((piece_rows, channels), jnp.bfloat16),
-        in_specs=[vmem],
+        in_specs=[smem] + [vmem] * team,
         out_specs=vmem,
         compiler_params=room,
-    )(pieces)
+    )(rank, *pieces)
 
 
 def solution(mesh):
@@ -377,6 +396,7 @@
             and BLOCK % (images // devices * CORES) == 0
             and channels % SHARE == 0
             and devices % (channels // SHARE * CORES) == 0
+            and (channels // SHARE) & (channels // SHARE - 1) == 0
         )
         return jax.shard_map(
             whole_shards if whole else shards,

time: 23.9 us -> 24.1 us (level)
  blocking collectives: 19.1 us -> 15.6 us
  starting transfers between devices: 1.15 us -> 3.13 us
  waiting for transfers between devices: 0.72 us -> 2.38 us
    all_to_all x1 -> x0, blocking collectives: 6.73 us -> none  [whole_shards(): lax.all_to_all(team_out.reshape(team, piece_rows, SHARE), AXES, split_axi...]
    all_to_all x1, blocking collectives: 12.3 us -> 15.6 us  [whole_shards(): lax.all_to_all(sent, AXES, split_axis=0, concat_axis=0, axis_index_groups...]
    ppermute x1 -> x3, starting transfers between devices: 1.15 us -> 3.13 us  [the longest x1 1.54 us: whole_shards(): their_start = lax.ppermute(mine[:, :middle], AXES, swap)]
    ppermute x1 -> x3, waiting for transfers between devices: 0.72 us -> 2.38 us  [the longest x1 1.73 us: whole_shards(): lax.ppermute(sent_piece, AXES, [(i, i ^ CORES * step + 1) for i in range(...]
    pallas_call x2 -> x3, Pallas kernels: 1.54 us -> 1.54 us  [the longest x1 0.7 us: whole_shards(): pl.pallas_call(functools.partial(whole_body, order, team, runs, emb_width...]
  transfers between devices with their start and end apart: 1 -> 3, of which waited for: 1 -> 2; matrix products, arithmetic and copies ran while one was open for 0% -> 0% of each run, Pallas kernels for 1% -> 4%
where the time goes in v7:
time: 24.1 us; the launch traced here: 23.9 us
  blocking collectives  15.6 us (65%)
  starting transfers between devices  3.13 us (13%)
  Pallas kernels  2.72 us (11%)
  waiting for transfers between devices  2.38 us (10%)
    all_to_all x1, blocking collectives, whole_shards(): lax.all_to_all(sent, AXES, split_axis=0, concat_axis=0, axis_index_groups...  15.6 us
    ppermute x1, waiting for transfers between devices, whole_shards(): lax.ppermute(sent_piece, AXES, [(i, i ^ CORES * step + 1) for i in range(...  1.73 us
    ppermute x1, starting transfers between devices, whole_shards(): their_start = lax.ppermute(mine[:, :middle], AXES, swap)  1.54 us
    ppermute x1, starting transfers between devices, whole_shards(): lax.ppermute(sent_piece, AXES, [(i, i ^ CORES * step + 1) for i in range(...  1.51 us
    pallas_call x1, Pallas kernels, whole_shards(): pl.pallas_call(functools.partial(pack_body, order), out_shape=(jax.ShapeD...  0.84 us
    pallas_call x1, Pallas kernels, whole_shards(): pl.pallas_call(functools.partial(whole_body, order, team, runs, emb_width...  0.7 us
    ppermute x1, waiting for transfers between devices, whole_shards(): their_start = lax.ppermute(mine[:, :middle], AXES, swap)  0.64 us
    pallas_call x1, Pallas kernels, whole_shards(): pl.pallas_call(place_body, out_shape=jax.ShapeDtypeStruct((piece_rows, ch...  0.62 us
  transfers between devices with their start and end apart: 3, of which 2 were waited for; matrix products, arithmetic and copies ran while one was open for 0% of the time, Pallas kernels for 4%

profile of v7, /device:TPU:0, one launch (start us, length us, event | category | flops | bytes accessed | tf_op | source)
XLA Modules:
  0.0 23.9 jit_solution(17710942608081059264)
XLA Ops:
  0.0 0.8 %shard_map.37 = (bf16[16,16,768]{2,1,0:T(8,128)(2,1)S(1)}, s32[2,2]{1,0:T(2,128)S(1)}) custom-call(bf16[16,256]{1,0:T(8,128)(2,1)} %emb_hbm.1, bf16[16,1024]{1,0:T(8,128)(2,1)} %lab_hbm.1, s32[2,2]{1,0:T(2,128)} %mask_hbm.1), custom_call_target="tpu_custom_call" | custom-call | tf_op jit(solution)/shard_map/pallas_call | solution.py:311
  0.8 15.6 %all_to_all.5 = bf16[16,16,768]{2,1,0:T(8,128)(2,1)S(1)} all-to-all(bf16[16,16,768]{2,1,0:T(8,128)(2,1)S(1)} %get-tuple-element.14), channel_id=1, replica_groups={{23,0,2,4,6,8,10,12,14,17,19,21,25,27,29,31},{22,1,3,5,7,9,11,13,15,16,..., dimensions={0} | all-to-all | bytes 786432 | tf_op jit(solution)/shard_map/all_to_all | solution.py:326
  16.5 1.5 %collective-permute-start = (bf16[256,384]{1,0:T(8,128)(2,1)S(1)}, bf16[256,384]{1,0:T(8,128)(2,1)S(1)}, u32[]{:S(2)}, u32[]{:S(2)}) collective-permute-start(bf16[256,384]{1,0:T(8,128)(2,1)S(1)} %get-tuple-element.22), channel_id=1, source_target_pairs={{0,1},{1,0},{2,3},{3,2},{4,5},{5,4},{6,7},{7,6},{8,9},{9,8},{10,11... | collective-permute-start | bytes 589832 | tf_op jit(solution)/shard_map/ppermute | solution.py:331
  18.0 0.1 collective-permute-start.1
  18.1 0.3 %shard_map.38 = (bf16[256,256]{1,0:T(8,128)(2,1)S(1)}, f32[256,128]{1,0:T(8,128)S(1)}) custom-call(s32[2,2]{1,0:T(2,128)S(1)} %get-tuple-element.13.kept_ref, bf16[256,768]{1,0:T(8,128)(2,1)S(1)} %bitcast.3), custom_call_target="tpu_custom_call" | custom-call | flops 33554432 | bytes 262144 | tf_op jit(solution)/shard_map/pallas_call | solution.py:333
  18.5 0.6 %collective-permute-done.start_ref = bf16[256,384]{1,0:T(8,128)(2,1)S(1)} collective-permute-done((bf16[256,384]{1,0:T(8,128)(2,1)S(1)}, bf16[256,384]{1,0:T(8,128)(2,1)S(1)}, u32[]{:S(2)}, u32[]{:S(2)}) %collective-permute-start) | collective-permute-done | bytes 196640 | tf_op jit(solution)/shard_map/ppermute | solution.py:331
  19.1 0.7 %shard_map.39 = (bf16[32,512]{1,0:T(8,128)(2,1)S(1)}, f32[512,128]{1,0:T(8,128)S(1)}) custom-call(s32[1]{0:T(128)} %bitcast.rank_ref, s32[2,2]{1,0:T(2,128)S(1)} %get-tuple-element.13.kept_ref, bf16[256,256]{1,0:T(8,128)(2,1)S(1)} %get-tuple-element.15.part_ref, f32[256,128]{1,0:T(8,128)S(1)} %get-tuple-element.16.sums_ref, bf16[256,768]{1,0:T(8,128)(2,1)S(1)} %bitcast.4, ...), custom_call_target="tpu_custom_call" | custom-call | flops 67108864 | bytes 524288 | tf_op jit(solution)/shard_map/pallas_call | solution.py:349
  19.8 0.0 collective-permute-done.1.end_ref
  19.8 0.2 shard_map.40
  20.1 1.5 %collective-permute-start.2 = (bf16[16,512]{1,0:T(8,128)(2,1)S(1)}, bf16[16,512]{1,0:T(8,128)(2,1)S(1)}, u32[]{:S(2)}, u32[]{:S(2)}) collective-permute-start(bf16[16,512]{1,0:T(8,128)(2,1)S(1)} %get-tuple-element.20), channel_id=1, source_target_pairs={{0,3},{1,2},{2,1},{3,0},{4,7},{5,6},{6,5},{7,4},{8,11},{9,10},{10,... | collective-permute-start | bytes 49160 | tf_op jit(solution)/shard_map/ppermute | solution.py:374
  21.6 1.7 %collective-permute-done.2.refs_1_ = bf16[16,512]{1,0:T(8,128)(2,1)S(1)} collective-permute-done((bf16[16,512]{1,0:T(8,128)(2,1)S(1)}, bf16[16,512]{1,0:T(8,128)(2,1)S(1)}, u32[]{:S(2)}, u32[]{:S(2)}) %collective-permute-start.2) | collective-permute-done | bytes 16416 | tf_op jit(solution)/shard_map/ppermute | solution.py:374
  23.3 0.6 %shard_map.41 = bf16[16,1024]{1,0:T(8,128)(2,1)} custom-call(s32[1]{0:T(128)} %bitcast.rank_ref, bf16[16,512]{1,0:T(8,128)(2,1)S(1)} %get-tuple-element.19.refs_0_, bf16[16,512]{1,0:T(8,128)(2,1)S(1)} %collective-permute-done.2.refs_1_), custom_call_target="tpu_custom_call" | custom-call | tf_op jit(solution)/shard_map/pallas_call | solution.py:377
  (1 shorter events, 0.0 us)
Async XLA Ops:
  16.5 2.6 %collective-permute-start = (bf16[256,384]{1,0:T(8,128)(2,1)S(1)}, bf16[256,384]{1,0:T(8,128)(2,1)S(1)}, u32[]{:S(2)}, u32[]{:S(2)}) collective-permute-start(bf16[256,384]{1,0:T(8,128)(2,1)S(1)} %get-tuple-element.22), channel_id=1, source_target_pairs={{0,1},{1,0},{2,3},{3,2},{4,5},{5,4},{6,7},{7,6},{8,9},{9,8},{10,11... | collective-permute-start | bytes 589832 | tf_op jit(solution)/shard_map/ppermute | solution.py:331
  18.0 1.8 %collective-permute-start.1 = (bf16[256,384]{1,0:T(8,128)(2,1)S(1)}, bf16[256,384]{1,0:T(8,128)(2,1)S(1)}, u32[]{:S(2)}, u32[]{:S(2)}) collective-permute-start(bf16[256,384]{1,0:T(8,128)(2,1)S(1)} %get-tuple-element.21), channel_id=1, source_target_pairs={{0,1},{1,0},{2,3},{3,2},{4,5},{5,4},{6,7},{7,6},{8,9},{9,8},{10,11... | collective-permute-start | bytes 589832 | tf_op jit(solution)/shard_map/ppermute | solution.py:332
  20.1 3.2 %collective-permute-start.2 = (bf16[16,512]{1,0:T(8,128)(2,1)S(1)}, bf16[16,512]{1,0:T(8,128)(2,1)S(1)}, u32[]{:S(2)}, u32[]{:S(2)}) collective-permute-start(bf16[16,512]{1,0:T(8,128)(2,1)S(1)} %get-tuple-element.20), channel_id=1, source_target_pairs={{0,3},{1,2},{2,1},{3,0},{4,7},{5,6},{6,5},{7,4},{8,11},{9,10},{10,... | collective-permute-start | bytes 49160 | tf_op jit(solution)/shard_map/ppermute | solution.py:374

commit v8 on v6

--- a/solution.py
+++ b/solution.py
@@ -238,21 +238,19 @@
     kernel_ref[half:, :half] = back
     kernel_ref[half:, half:] = theirs
     degrees[0] = degrees[0] + row_sums(across)
-    degrees[1] = jnp.broadcast_to(row_sums(back) + row_sums(theirs), (half, share))
+    degrees[1] = jnp.broadcast_to(
+        jnp.sum(back.astype(jnp.float32) + theirs.astype(jnp.float32), axis=1, keepdims=True),
+        (half, share),
+    )
+    inv_root = lax.rsqrt(jnp.concatenate(degrees, axis=0))
+    root_ref[...] = inv_root
     labels = jnp.concatenate([mine_ref[:, emb_width:], theirs_ref[:, emb_width:]], axis=0).astype(
         jnp.float32
     )
-    weights = kernel_ref[...]
-    inv_root = lax.rsqrt(jnp.concatenate(degrees, axis=0))
-    root_ref[...] = MIXING * inv_root
-    kept_part = (1.0 - MIXING) * labels
-    label_ref[...] = kept_part
-    current = labels
-    for iteration in range(ITERS - 1):
-        scaled = (inv_root * current).astype(jnp.bfloat16)
-        spread = jnp.dot(weights, scaled, preferred_element_type=jnp.float32)
-        current = MIXING * inv_root * spread + kept_part
-    scaled = (inv_root * current).astype(jnp.bfloat16)
+    label_ref[...] = (1.0 - MIXING) * labels
+    scaled = (inv_root * labels).astype(jnp.bfloat16)
+    shares = jnp.concatenate([inv_root * inv_root] * (2 * half // share), axis=1)
+    passed = (shares * kernel_ref[...].astype(jnp.float32)).astype(jnp.bfloat16)
     chip, core = rank_ref[0] // CORES, rank_ref[0] % CORES
     gather_side = core ^ gather_flip(chip, chips)
     team_side = core ^ team_flip(chip, chips)
@@ -263,10 +261,17 @@
         place = jnp.where(target == order[0], 0, target + 1 * (target < order[0]))
         row = place * piece + half * (side ^ gather_side)
         own.append(pl.ds(pl.multiple_of(row, 16), piece))
-    own_weights = jnp.concatenate([kernel_ref[rows, :] for rows in own], axis=0)
+    first = MIXING * jnp.concatenate([kernel_ref[rows, :] for rows in own], axis=0).astype(
+        jnp.float32
+    )
     own_labels = jnp.concatenate([label_ref[rows, :] for rows in own], axis=0)
     own_root = jnp.concatenate([root_ref[rows, :] for rows in own], axis=0)
-    spread = jnp.dot(own_weights, scaled, preferred_element_type=jnp.float32)
+    steps = first
+    for iteration in range(ITERS - 1):
+        steps = MIXING * jnp.dot(
+            steps.astype(jnp.bfloat16), passed, preferred_element_type=jnp.float32
+        ) + (1.0 - MIXING) * first
+    spread = jnp.dot(steps.astype(jnp.bfloat16), scaled, preferred_element_type=jnp.float32)
     out_ref[...] = (own_root * spread + own_labels).astype(jnp.bfloat16)
 
 

time: 23.9 us -> 23.8 us (level)
  no operation moved by 1% of the time
where the time goes in v8:
time: 23.8 us; the launch traced here: 23.6 us
  blocking collectives  19 us (80%)
  Pallas kernels  2.62 us (11%)
  starting transfers between devices  1.15 us (5%)
  waiting for transfers between devices  0.72 us (3%)
    all_to_all x1, blocking collectives, whole_shards(): lax.all_to_all(sent, AXES, split_axis=0, concat_axis=0, axis_index_groups...  12.3 us
    all_to_all x1, blocking collectives, whole_shards(): lax.all_to_all(team_out.reshape(team, piece_rows, SHARE), AXES, split_axi...  6.72 us
    ppermute x1, starting transfers between devices, whole_shards(): theirs = lax.ppermute(mine, AXES, [(i, i ^ 1) for i in range(devices)])  1.15 us
    pallas_call x1, Pallas kernels, whole_shards(): pl.pallas_call(functools.partial(pack_body, order), out_shape=(jax.ShapeD...  0.83 us
    pallas_call x1, Pallas kernels, whole_shards(): pl.pallas_call(functools.partial(spread_body, emb_width, order, ranks, ru...  0.83 us
    ppermute x1, waiting for transfers between devices, whole_shards(): theirs = lax.ppermute(mine, AXES, [(i, i ^ 1) for i in range(devices)])  0.72 us
    pallas_call x1, Pallas kernels, whole_shards(): pl.pallas_call(functools.partial(place_body, ranks), out_shape=jax.ShapeD...  0.62 us
  transfers between devices with their start and end apart: 1, of which 1 were waited for; matrix products, arithmetic and copies ran while one was open for 0% of the time, Pallas kernels for 1%

profile of v8, /device:TPU:0, one launch (start us, length us, event | category | flops | bytes accessed | tf_op | source)
XLA Modules:
  0.0 23.6 jit_solution(13732160626747660645)
XLA Ops:
  0.0 0.8 %shard_map.37 = (bf16[16,16,384]{2,1,0:T(8,128)(2,1)S(1)}, s32[2,2]{1,0:T(2,128)S(1)}) custom-call(bf16[16,256]{1,0:T(8,128)(2,1)} %emb_hbm.1, bf16[16,1024]{1,0:T(8,128)(2,1)} %lab_hbm.1, s32[2,2]{1,0:T(2,128)} %mask_hbm.1), custom_call_target="tpu_custom_call" | custom-call | tf_op jit(solution)/shard_map/pallas_call | solution.py:308
  0.8 12.3 %all_to_all.10 = bf16[16,16,384]{2,1,0:T(8,128)(2,1)S(1)} all-to-all(bf16[16,16,384]{2,1,0:T(8,128)(2,1)S(1)} %get-tuple-element.10), channel_id=1, replica_groups={{23,0,2,4,6,8,10,12,14,17,19,21,25,27,29,31},{22,1,3,5,7,9,11,13,15,16,..., dimensions={0} | all-to-all | bytes 393216 | tf_op jit(solution)/shard_map/all_to_all | solution.py:323
  13.2 1.2 %collective-permute-start = (bf16[256,384]{1,0:T(8,128)(2,1)S(1)}, bf16[256,384]{1,0:T(8,128)(2,1)S(1)}, u32[]{:S(2)}, u32[]{:S(2)}) collective-permute-start(bf16[256,384]{1,0:T(8,128)(2,1)S(1)} %bitcast.3), channel_id=1, source_target_pairs={{0,1},{1,0},{2,3},{3,2},{4,5},{5,4},{6,7},{7,6},{8,9},{9,8},{10,11... | collective-permute-start | bytes 589832 | tf_op jit(solution)/shard_map/ppermute | solution.py:326
  14.3 0.3 %shard_map.38 = (bf16[256,256]{1,0:T(8,128)(2,1)S(1)}, f32[256,128]{1,0:T(8,128)S(1)}) custom-call(s32[2,2]{1,0:T(2,128)S(1)} %get-tuple-element.9.kept_ref, bf16[256,384]{1,0:T(8,128)(2,1)S(1)} %bitcast.4), custom_call_target="tpu_custom_call" | custom-call | flops 33554432 | bytes 262144 | tf_op jit(solution)/shard_map/pallas_call | solution.py:327
  14.7 0.7 %collective-permute-done.theirs_ref = bf16[256,384]{1,0:T(8,128)(2,1)S(1)} collective-permute-done((bf16[256,384]{1,0:T(8,128)(2,1)S(1)}, bf16[256,384]{1,0:T(8,128)(2,1)S(1)}, u32[]{:S(2)}, u32[]{:S(2)}) %collective-permute-start) | collective-permute-done | bytes 196640 | tf_op jit(solution)/shard_map/ppermute | solution.py:326
  15.4 0.8 %shard_map.39 = bf16[128,128]{1,0:T(8,128)(2,1)S(1)} custom-call(s32[1]{0:T(128)} %bitcast.rank_ref, s32[2,2]{1,0:T(2,128)S(1)} %get-tuple-element.9.kept_ref, bf16[256,256]{1,0:T(8,128)(2,1)S(1)} %get-tuple-element.11.part_ref, f32[256,128]{1,0:T(8,128)S(1)} %get-tuple-element.12.sums_ref, bf16[256,384]{1,0:T(8,128)(2,1)S(1)} %bitcast.5, ...), custom_call_target="tpu_custom_call" | custom-call | tf_op jit(solution)/shard_map/pallas_call | solution.py:343
  16.2 6.7 %all_to_all.11.pieces_ref = bf16[8,16,128]{2,1,0:T(8,128)(2,1)S(1)} all-to-all(bf16[8,16,128]{2,1,0:T(8,128)(2,1)S(1)} %bitcast.6), channel_id=1, replica_groups={{15,0,3,5,7,9,11,13},{14,1,2,4,6,8,10,12},{30,16,18,20,22,24,26,28},{31..., dimensions={0} | all-to-all | bytes 65536 | tf_op jit(solution)/shard_map/all_to_all | solution.py:355
  22.9 0.6 %shard_map.40 = bf16[16,1024]{1,0:T(8,128)(2,1)} custom-call(bf16[8,16,128]{2,1,0:T(8,128)(2,1)S(1)} %all_to_all.11.pieces_ref), custom_call_target="tpu_custom_call" | custom-call | tf_op jit(solution)/shard_map/pallas_call | solution.py:363
Async XLA Ops:
  13.2 2.2 %collective-permute-start = (bf16[256,384]{1,0:T(8,128)(2,1)S(1)}, bf16[256,384]{1,0:T(8,128)(2,1)S(1)}, u32[]{:S(2)}, u32[]{:S(2)}) collective-permute-start(bf16[256,384]{1,0:T(8,128)(2,1)S(1)} %bitcast.3), channel_id=1, source_target_pairs={{0,1},{1,0},{2,3},{3,2},{4,5},{5,4},{6,7},{7,6},{8,9},{9,8},{10,11... | collective-permute-start | bytes 589832 | tf_op jit(solution)/shard_map/ppermute | solution.py:326

commit v9 on v6

--- a/solution.py
+++ b/solution.py
@@ -238,7 +238,10 @@
     kernel_ref[half:, :half] = back
     kernel_ref[half:, half:] = theirs
     degrees[0] = degrees[0] + row_sums(across)
-    degrees[1] = jnp.broadcast_to(row_sums(back) + row_sums(theirs), (half, share))
+    degrees[1] = jnp.broadcast_to(
+        jnp.sum(back.astype(jnp.float32) + theirs.astype(jnp.float32), axis=1, keepdims=True),
+        (half, share),
+    )
     labels = jnp.concatenate([mine_ref[:, emb_width:], theirs_ref[:, emb_width:]], axis=0).astype(
         jnp.float32
     )

time: 23.9 us -> 23.9 us (level)
  no operation moved by 1% of the time
where the time goes in v9:
time: 23.9 us; the launch traced here: 23.6 us
  blocking collectives  19.1 us (80%)
  Pallas kernels  2.68 us (11%)
  starting transfers between devices  1.15 us (5%)
  waiting for transfers between devices  0.72 us (3%)
    all_to_all x1, blocking collectives, whole_shards(): lax.all_to_all(sent, AXES, split_axis=0, concat_axis=0, axis_index_groups...  12.3 us
    all_to_all x1, blocking collectives, whole_shards(): lax.all_to_all(team_out.reshape(team, piece_rows, SHARE), AXES, split_axi...  6.73 us
    ppermute x1, starting transfers between devices, whole_shards(): theirs = lax.ppermute(mine, AXES, [(i, i ^ 1) for i in range(devices)])  1.15 us
    pallas_call x1, Pallas kernels, whole_shards(): pl.pallas_call(functools.partial(spread_body, emb_width, order, ranks, ru...  0.89 us
    pallas_call x1, Pallas kernels, whole_shards(): pl.pallas_call(functools.partial(pack_body, order), out_shape=(jax.ShapeD...  0.83 us
    ppermute x1, waiting for transfers between devices, whole_shards(): theirs = lax.ppermute(mine, AXES, [(i, i ^ 1) for i in range(devices)])  0.72 us
    pallas_call x1, Pallas kernels, whole_shards(): pl.pallas_call(functools.partial(place_body, ranks), out_shape=jax.ShapeD...  0.62 us
  transfers between devices with their start and end apart: 1, of which 1 were waited for; matrix products, arithmetic and copies ran while one was open for 0% of the time, Pallas kernels for 1%

profile of v9, /device:TPU:0, one launch (start us, length us, event | category | flops | bytes accessed | tf_op | source)
XLA Modules:
  0.0 23.6 jit_solution(2982945889133297958)
XLA Ops:
  0.0 0.8 %shard_map.37 = (bf16[16,16,384]{2,1,0:T(8,128)(2,1)S(1)}, s32[2,2]{1,0:T(2,128)S(1)}) custom-call(bf16[16,256]{1,0:T(8,128)(2,1)} %emb_hbm.1, bf16[16,1024]{1,0:T(8,128)(2,1)} %lab_hbm.1, s32[2,2]{1,0:T(2,128)} %mask_hbm.1), custom_call_target="tpu_custom_call" | custom-call | tf_op jit(solution)/shard_map/pallas_call | solution.py:306
  0.8 12.3 %all_to_all.10 = bf16[16,16,384]{2,1,0:T(8,128)(2,1)S(1)} all-to-all(bf16[16,16,384]{2,1,0:T(8,128)(2,1)S(1)} %get-tuple-element.10), channel_id=1, replica_groups={{23,0,2,4,6,8,10,12,14,17,19,21,25,27,29,31},{22,1,3,5,7,9,11,13,15,16,..., dimensions={0} | all-to-all | bytes 393216 | tf_op jit(solution)/shard_map/all_to_all | solution.py:321
  13.2 1.2 %collective-permute-start = (bf16[256,384]{1,0:T(8,128)(2,1)S(1)}, bf16[256,384]{1,0:T(8,128)(2,1)S(1)}, u32[]{:S(2)}, u32[]{:S(2)}) collective-permute-start(bf16[256,384]{1,0:T(8,128)(2,1)S(1)} %bitcast.3), channel_id=1, source_target_pairs={{0,1},{1,0},{2,3},{3,2},{4,5},{5,4},{6,7},{7,6},{8,9},{9,8},{10,11... | collective-permute-start | bytes 589832 | tf_op jit(solution)/shard_map/ppermute | solution.py:324
  14.3 0.3 %shard_map.38 = (bf16[256,256]{1,0:T(8,128)(2,1)S(1)}, f32[256,128]{1,0:T(8,128)S(1)}) custom-call(s32[2,2]{1,0:T(2,128)S(1)} %get-tuple-element.9.kept_ref, bf16[256,384]{1,0:T(8,128)(2,1)S(1)} %bitcast.4), custom_call_target="tpu_custom_call" | custom-call | flops 33554432 | bytes 262144 | tf_op jit(solution)/shard_map/pallas_call | solution.py:325
  14.7 0.7 %collective-permute-done.theirs_ref = bf16[256,384]{1,0:T(8,128)(2,1)S(1)} collective-permute-done((bf16[256,384]{1,0:T(8,128)(2,1)S(1)}, bf16[256,384]{1,0:T(8,128)(2,1)S(1)}, u32[]{:S(2)}, u32[]{:S(2)}) %collective-permute-start) | collective-permute-done | bytes 196640 | tf_op jit(solution)/shard_map/ppermute | solution.py:324
  15.4 0.9 %shard_map.39 = bf16[128,128]{1,0:T(8,128)(2,1)S(1)} custom-call(s32[1]{0:T(128)} %bitcast.rank_ref, s32[2,2]{1,0:T(2,128)S(1)} %get-tuple-element.9.kept_ref, bf16[256,256]{1,0:T(8,128)(2,1)S(1)} %get-tuple-element.11.part_ref, f32[256,128]{1,0:T(8,128)S(1)} %get-tuple-element.12.sums_ref, bf16[256,384]{1,0:T(8,128)(2,1)S(1)} %bitcast.5, ...), custom_call_target="tpu_custom_call" | custom-call | tf_op jit(solution)/shard_map/pallas_call | solution.py:341
  16.3 6.7 %all_to_all.11.pieces_ref = bf16[8,16,128]{2,1,0:T(8,128)(2,1)S(1)} all-to-all(bf16[8,16,128]{2,1,0:T(8,128)(2,1)S(1)} %bitcast.6), channel_id=1, replica_groups={{15,0,3,5,7,9,11,13},{14,1,2,4,6,8,10,12},{30,16,18,20,22,24,26,28},{31..., dimensions={0} | all-to-all | bytes 65536 | tf_op jit(solution)/shard_map/all_to_all | solution.py:353
  23.0 0.6 %shard_map.40 = bf16[16,1024]{1,0:T(8,128)(2,1)} custom-call(bf16[8,16,128]{2,1,0:T(8,128)(2,1)S(1)} %all_to_all.11.pieces_ref), custom_call_target="tpu_custom_call" | custom-call | tf_op jit(solution)/shard_map/pallas_call | solution.py:361
Async XLA Ops:
  13.2 2.2 %collective-permute-start = (bf16[256,384]{1,0:T(8,128)(2,1)S(1)}, bf16[256,384]{1,0:T(8,128)(2,1)S(1)}, u32[]{:S(2)}, u32[]{:S(2)}) collective-permute-start(bf16[256,384]{1,0:T(8,128)(2,1)S(1)} %bitcast.3), channel_id=1, source_target_pairs={{0,1},{1,0},{2,3},{3,2},{4,5},{5,4},{6,7},{7,6},{8,9},{9,8},{10,11... | collective-permute-start | bytes 589832 | tf_op jit(solution)/shard_map/ppermute | solution.py:324

commit v10 on v9

--- a/solution.py
+++ b/solution.py
@@ -139,7 +139,8 @@
 
 
 def team_order(team):
-    return [team - 1] + list(range(team - 1))
+    planes = [rank for pair in zip(range(team // 2), range(team // 2, team)) for rank in pair]
+    return [team - 1] + planes[:-1]
 
 
 def gather_flip(chip, chips):

time: 23.9 us -> 23.8 us (level)
  no operation moved by 1% of the time
where the time goes in v10:
time: 23.8 us; the launch traced here: 23.6 us
  blocking collectives  19 us (80%)
  Pallas kernels  2.68 us (11%)
  starting transfers between devices  1.15 us (5%)
  waiting for transfers between devices  0.72 us (3%)
    all_to_all x1, blocking collectives, whole_shards(): lax.all_to_all(sent, AXES, split_axis=0, concat_axis=0, axis_index_groups...  12.3 us
    all_to_all x1, blocking collectives, whole_shards(): lax.all_to_all(team_out.reshape(team, piece_rows, SHARE), AXES, split_axi...  6.69 us
    ppermute x1, starting transfers between devices, whole_shards(): theirs = lax.ppermute(mine, AXES, [(i, i ^ 1) for i in range(devices)])  1.15 us
    pallas_call x1, Pallas kernels, whole_shards(): pl.pallas_call(functools.partial(spread_body, emb_width, order, ranks, ru...  0.89 us
    pallas_call x1, Pallas kernels, whole_shards(): pl.pallas_call(functools.partial(pack_body, order), out_shape=(jax.ShapeD...  0.83 us
    ppermute x1, waiting for transfers between devices, whole_shards(): theirs = lax.ppermute(mine, AXES, [(i, i ^ 1) for i in range(devices)])  0.72 us
    pallas_call x1, Pallas kernels, whole_shards(): pl.pallas_call(functools.partial(place_body, ranks), out_shape=jax.ShapeD...  0.62 us
  transfers between devices with their start and end apart: 1, of which 1 were waited for; matrix products, arithmetic and copies ran while one was open for 0% of the time, Pallas kernels for 1%

profile of v10, /device:TPU:0, one launch (start us, length us, event | category | flops | bytes accessed | tf_op | source)
XLA Modules:
  0.0 23.6 jit_solution(15117614902938606711)
XLA Ops:
  0.0 0.8 %shard_map.37 = (bf16[16,16,384]{2,1,0:T(8,128)(2,1)S(1)}, s32[2,2]{1,0:T(2,128)S(1)}) custom-call(bf16[16,256]{1,0:T(8,128)(2,1)} %emb_hbm.1, bf16[16,1024]{1,0:T(8,128)(2,1)} %lab_hbm.1, s32[2,2]{1,0:T(2,128)} %mask_hbm.1), custom_call_target="tpu_custom_call" | custom-call | tf_op jit(solution)/shard_map/pallas_call | solution.py:307
  0.8 12.3 %all_to_all.10 = bf16[16,16,384]{2,1,0:T(8,128)(2,1)S(1)} all-to-all(bf16[16,16,384]{2,1,0:T(8,128)(2,1)S(1)} %get-tuple-element.10), channel_id=1, replica_groups={{23,0,2,4,6,8,10,12,14,17,19,21,25,27,29,31},{22,1,3,5,7,9,11,13,15,16,..., dimensions={0} | all-to-all | bytes 393216 | tf_op jit(solution)/shard_map/all_to_all | solution.py:322
  13.2 1.2 %collective-permute-start = (bf16[256,384]{1,0:T(8,128)(2,1)S(1)}, bf16[256,384]{1,0:T(8,128)(2,1)S(1)}, u32[]{:S(2)}, u32[]{:S(2)}) collective-permute-start(bf16[256,384]{1,0:T(8,128)(2,1)S(1)} %bitcast.3), channel_id=1, source_target_pairs={{0,1},{1,0},{2,3},{3,2},{4,5},{5,4},{6,7},{7,6},{8,9},{9,8},{10,11... | collective-permute-start | bytes 589832 | tf_op jit(solution)/shard_map/ppermute | solution.py:325
  14.3 0.3 %shard_map.38 = (bf16[256,256]{1,0:T(8,128)(2,1)S(1)}, f32[256,128]{1,0:T(8,128)S(1)}) custom-call(s32[2,2]{1,0:T(2,128)S(1)} %get-tuple-element.9.kept_ref, bf16[256,384]{1,0:T(8,128)(2,1)S(1)} %bitcast.4), custom_call_target="tpu_custom_call" | custom-call | flops 33554432 | bytes 262144 | tf_op jit(solution)/shard_map/pallas_call | solution.py:326
  14.7 0.7 %collective-permute-done.theirs_ref = bf16[256,384]{1,0:T(8,128)(2,1)S(1)} collective-permute-done((bf16[256,384]{1,0:T(8,128)(2,1)S(1)}, bf16[256,384]{1,0:T(8,128)(2,1)S(1)}, u32[]{:S(2)}, u32[]{:S(2)}) %collective-permute-start) | collective-permute-done | bytes 196640 | tf_op jit(solution)/shard_map/ppermute | solution.py:325
  15.4 0.9 %shard_map.39 = bf16[128,128]{1,0:T(8,128)(2,1)S(1)} custom-call(s32[1]{0:T(128)} %bitcast.rank_ref, s32[2,2]{1,0:T(2,128)S(1)} %get-tuple-element.9.kept_ref, bf16[256,256]{1,0:T(8,128)(2,1)S(1)} %get-tuple-element.11.part_ref, f32[256,128]{1,0:T(8,128)S(1)} %get-tuple-element.12.sums_ref, bf16[256,384]{1,0:T(8,128)(2,1)S(1)} %bitcast.5, ...), custom_call_target="tpu_custom_call" | custom-call | tf_op jit(solution)/shard_map/pallas_call | solution.py:342
  16.3 6.7 %all_to_all.11.pieces_ref = bf16[8,16,128]{2,1,0:T(8,128)(2,1)S(1)} all-to-all(bf16[8,16,128]{2,1,0:T(8,128)(2,1)S(1)} %bitcast.6), channel_id=1, replica_groups={{15,0,9,3,11,5,13,7},{14,1,8,2,10,4,12,6},{30,16,24,18,26,20,28,22},{31..., dimensions={0} | all-to-all | bytes 65536 | tf_op jit(solution)/shard_map/all_to_all | solution.py:354
  23.0 0.6 %shard_map.40 = bf16[16,1024]{1,0:T(8,128)(2,1)} custom-call(bf16[8,16,128]{2,1,0:T(8,128)(2,1)S(1)} %all_to_all.11.pieces_ref), custom_call_target="tpu_custom_call" | custom-call | tf_op jit(solution)/shard_map/pallas_call | solution.py:362
Async XLA Ops:
  13.2 2.2 %collective-permute-start = (bf16[256,384]{1,0:T(8,128)(2,1)S(1)}, bf16[256,384]{1,0:T(8,128)(2,1)S(1)}, u32[]{:S(2)}, u32[]{:S(2)}) collective-permute-start(bf16[256,384]{1,0:T(8,128)(2,1)S(1)} %bitcast.3), channel_id=1, source_target_pairs={{0,1},{1,0},{2,3},{3,2},{4,5},{5,4},{6,7},{7,6},{8,9},{9,8},{10,11... | collective-permute-start | bytes 589832 | tf_op jit(solution)/shard_map/ppermute | solution.py:325

commit v11 on v8

--- a/solution.py
+++ b/solution.py
@@ -249,8 +249,17 @@
     )
     label_ref[...] = (1.0 - MIXING) * labels
     scaled = (inv_root * labels).astype(jnp.bfloat16)
-    shares = jnp.concatenate([inv_root * inv_root] * (2 * half // share), axis=1)
-    passed = (shares * kernel_ref[...].astype(jnp.float32)).astype(jnp.bfloat16)
+    shares = [inv_root[side * half : (side + 1) * half] for side in range(2)]
+    shares = [jnp.concatenate([part * part] * (half // share), axis=1) for part in shares]
+    passed = jnp.concatenate(
+        [
+            jnp.concatenate(
+                [(shares[row] * part.astype(jnp.float32)).astype(jnp.bfloat16) for part in line], axis=1
+            )
+            for row, line in enumerate(((part_ref[...], across), (back, theirs)))
+        ],
+        axis=0,
+    )
     chip, core = rank_ref[0] // CORES, rank_ref[0] % CORES
     gather_side = core ^ gather_flip(chip, chips)
     team_side = core ^ team_flip(chip, chips)

time: 23.8 us -> 23.8 us (level)
  no operation moved by 1% of the time
where the time goes in v11:
time: 23.8 us; the launch traced here: 23.6 us
  blocking collectives  19.1 us (80%)
  Pallas kernels  2.63 us (11%)
  starting transfers between devices  1.15 us (5%)
  waiting for transfers between devices  0.72 us (3%)
    all_to_all x1, blocking collectives, whole_shards(): lax.all_to_all(sent, AXES, split_axis=0, concat_axis=0, axis_index_groups...  12.3 us
    all_to_all x1, blocking collectives, whole_shards(): lax.all_to_all(team_out.reshape(team, piece_rows, SHARE), AXES, split_axi...  6.73 us
    ppermute x1, starting transfers between devices, whole_shards(): theirs = lax.ppermute(mine, AXES, [(i, i ^ 1) for i in range(devices)])  1.15 us
    pallas_call x1, Pallas kernels, whole_shards(): pl.pallas_call(functools.partial(spread_body, emb_width, order, ranks, ru...  0.84 us
    pallas_call x1, Pallas kernels, whole_shards(): pl.pallas_call(functools.partial(pack_body, order), out_shape=(jax.ShapeD...  0.83 us
    ppermute x1, waiting for transfers between devices, whole_shards(): theirs = lax.ppermute(mine, AXES, [(i, i ^ 1) for i in range(devices)])  0.72 us
    pallas_call x1, Pallas kernels, whole_shards(): pl.pallas_call(functools.partial(place_body, ranks), out_shape=jax.ShapeD...  0.62 us
  transfers between devices with their start and end apart: 1, of which 1 were waited for; matrix products, arithmetic and copies ran while one was open for 0% of the time, Pallas kernels for 1%

profile of v11, /device:TPU:0, one launch (start us, length us, event | category | flops | bytes accessed | tf_op | source)
XLA Modules:
  0.0 23.6 jit_solution(2257851749849472921)
XLA Ops:
  0.0 0.8 %shard_map.37 = (bf16[16,16,384]{2,1,0:T(8,128)(2,1)S(1)}, s32[2,2]{1,0:T(2,128)S(1)}) custom-call(bf16[16,256]{1,0:T(8,128)(2,1)} %emb_hbm.1, bf16[16,1024]{1,0:T(8,128)(2,1)} %lab_hbm.1, s32[2,2]{1,0:T(2,128)} %mask_hbm.1), custom_call_target="tpu_custom_call" | custom-call | tf_op jit(solution)/shard_map/pallas_call | solution.py:317
  0.8 12.3 %all_to_all.10 = bf16[16,16,384]{2,1,0:T(8,128)(2,1)S(1)} all-to-all(bf16[16,16,384]{2,1,0:T(8,128)(2,1)S(1)} %get-tuple-element.10), channel_id=1, replica_groups={{23,0,2,4,6,8,10,12,14,17,19,21,25,27,29,31},{22,1,3,5,7,9,11,13,15,16,..., dimensions={0} | all-to-all | bytes 393216 | tf_op jit(solution)/shard_map/all_to_all | solution.py:332
  13.2 1.2 %collective-permute-start = (bf16[256,384]{1,0:T(8,128)(2,1)S(1)}, bf16[256,384]{1,0:T(8,128)(2,1)S(1)}, u32[]{:S(2)}, u32[]{:S(2)}) collective-permute-start(bf16[256,384]{1,0:T(8,128)(2,1)S(1)} %bitcast.3), channel_id=1, source_target_pairs={{0,1},{1,0},{2,3},{3,2},{4,5},{5,4},{6,7},{7,6},{8,9},{9,8},{10,11... | collective-permute-start | bytes 589832 | tf_op jit(solution)/shard_map/ppermute | solution.py:335
  14.3 0.3 %shard_map.38 = (bf16[256,256]{1,0:T(8,128)(2,1)S(1)}, f32[256,128]{1,0:T(8,128)S(1)}) custom-call(s32[2,2]{1,0:T(2,128)S(1)} %get-tuple-element.9.kept_ref, bf16[256,384]{1,0:T(8,128)(2,1)S(1)} %bitcast.4), custom_call_target="tpu_custom_call" | custom-call | flops 33554432 | bytes 262144 | tf_op jit(solution)/shard_map/pallas_call | solution.py:336
  14.7 0.7 %collective-permute-done.theirs_ref = bf16[256,384]{1,0:T(8,128)(2,1)S(1)} collective-permute-done((bf16[256,384]{1,0:T(8,128)(2,1)S(1)}, bf16[256,384]{1,0:T(8,128)(2,1)S(1)}, u32[]{:S(2)}, u32[]{:S(2)}) %collective-permute-start) | collective-permute-done | bytes 196640 | tf_op jit(solution)/shard_map/ppermute | solution.py:335
  15.4 0.8 %shard_map.39 = bf16[128,128]{1,0:T(8,128)(2,1)S(1)} custom-call(s32[1]{0:T(128)} %bitcast.rank_ref, s32[2,2]{1,0:T(2,128)S(1)} %get-tuple-element.9.kept_ref, bf16[256,256]{1,0:T(8,128)(2,1)S(1)} %get-tuple-element.11.part_ref, f32[256,128]{1,0:T(8,128)S(1)} %get-tuple-element.12.sums_ref, bf16[256,384]{1,0:T(8,128)(2,1)S(1)} %bitcast.5, ...), custom_call_target="tpu_custom_call" | custom-call | tf_op jit(solution)/shard_map/pallas_call | solution.py:352
  16.2 6.7 %all_to_all.11.pieces_ref = bf16[8,16,128]{2,1,0:T(8,128)(2,1)S(1)} all-to-all(bf16[8,16,128]{2,1,0:T(8,128)(2,1)S(1)} %bitcast.6), channel_id=1, replica_groups={{15,0,3,5,7,9,11,13},{14,1,2,4,6,8,10,12},{30,16,18,20,22,24,26,28},{31..., dimensions={0} | all-to-all | bytes 65536 | tf_op jit(solution)/shard_map/all_to_all | solution.py:364
  23.0 0.6 %shard_map.40 = bf16[16,1024]{1,0:T(8,128)(2,1)} custom-call(bf16[8,16,128]{2,1,0:T(8,128)(2,1)S(1)} %all_to_all.11.pieces_ref), custom_call_target="tpu_custom_call" | custom-call | tf_op jit(solution)/shard_map/pallas_call | solution.py:372
Async XLA Ops:
  13.2 2.2 %collective-permute-start = (bf16[256,384]{1,0:T(8,128)(2,1)S(1)}, bf16[256,384]{1,0:T(8,128)(2,1)S(1)}, u32[]{:S(2)}, u32[]{:S(2)}) collective-permute-start(bf16[256,384]{1,0:T(8,128)(2,1)S(1)} %bitcast.3), channel_id=1, source_target_pairs={{0,1},{1,0},{2,3},{3,2},{4,5},{5,4},{6,7},{7,6},{8,9},{9,8},{10,11... | collective-permute-start | bytes 589832 | tf_op jit(solution)/shard_map/ppermute | solution.py:335
